TPU v7x, 32 devices: a whole 2x2x4 slice. The times are simulated.
32 devices in a mesh: tu: 8 (over z, x), tv: 4 (over y, core).
Axes of the slice: x: 2, y: 2, z: 4, core: 2. Of those that a mesh axis runs over, the one named last changes fastest.
Arguments:
- aperture_amp: bfloat16 [128, 512, 512], P(('tu', 'tv')), may hold values from 0.19921875 to 1.796875
- aperture_phase: bfloat16 [128, 512, 512], P(('tu', 'tv')), may hold values from -3.140625 to 3.140625
- plane_depths: float32 [4], replicated, may hold values from 8 to 344
- send_list: int32 [32, 32, 2], P(('tu', 'tv')), may hold values from 0 to 15, as said below
- send_count: int32 [32, 32], P(('tu', 'tv')), may hold values from 0 to 2, as said below
- vis_left: bfloat16 [12288, 128, 128], P(('tu', 'tv')), may hold values from -0.078125 to 0.078125
- vis_right: bfloat16 [12288, 64, 128], P(('tu', 'tv')), may hold values from -0.75 to 0.75
- block_slot: int32 [12288], P(('tu', 'tv')), may hold values from 0 to 63, as said below
- block_pos: int32 [12288], P(('tu', 'tv')), may hold values from 0 to 31
- block_count: int32 [32], P(('tu', 'tv')), may hold values from 96 to 384, as said below
Outputs:
- uv_grid: float32 [2, 2048, 2048], P(None, 'tu', 'tv')
Inputs may be any that keep to these rules, and one draw needn't show every extreme that they name: `send_list`: each owner sends every one of its kernels to 2 slots, 32 in all; the used slots of an owner and tile are the first send_count of them; entries of unused slots are arbitrary kernel numbers in range. One tile, drawn afresh, receives 2 slots from every owner; a row of send_count sums to 32. `block_slot`: names a slot r = d * 2 + c that the block's tile receives, with c < send_count[d, tile]. `block_count`: some tile uses all 384 slots.
All inputs are finite; a program needn't handle non-finite values.
Results may differ from a plain program's by a relative error of at most 0.0065.
Values may be sent and summed in bfloat16 or wider, within the bound.
No kernel may reach another device: no remote copies, remote signals or barrier semaphores. Data moves between devices by JAX's collectives and lax.ppermute only.
A program may use at most 192 MiB of HBM per device.

v0:
```python
import functools
import math

import jax
import jax.numpy as jnp
import numpy as np
from jax import lax
from jax.experimental import pallas as pl
from jax.experimental.pallas import tpu as pltpu
from jax.sharding import PartitionSpec as P

TILE_U = 256
TILE_V = 512
QUAD = 4
UNROLL = 4
STEP = 2 * UNROLL
RING = 4

def _fit(fn, degree):
    span = math.pi ** 2
    nodes = 0.5 * span * (1.0 - np.cos(np.pi * (np.arange(400) + 0.5) / 400))
    cheb = np.polynomial.chebyshev.Chebyshev.fit(nodes, fn(np.sqrt(nodes)), degree, domain=[0, span])
    return [float(c) for c in cheb.convert(kind=np.polynomial.Polynomial).coef]


COS_POLY = _fit(np.cos, 6)
SIN_POLY = _fit(lambda x: np.sin(x) / x, 5)


def horner(coefs, u):
    total = jnp.full_like(u, coefs[-1])
    for coef in coefs[-2::-1]:
        total = total * u + coef
    return total


def cos_sin(x):
    u = x * x
    return horner(COS_POLY, u), x * horner(SIN_POLY, u)


def from_behind(block, axis, distance):
    devices = range(lax.axis_size(axis))
    route = [(i - distance, i) for i in devices if i - distance in devices]
    return lax.ppermute(block, axis, route)


def in_hbm(array):
    return pltpu.with_memory_space_constraint(array, pltpu.HBM)


def in_vmem(array):
    return pltpu.with_memory_space_constraint(array, pltpu.VMEM)


def in_smem(array):
    return pltpu.with_memory_space_constraint(array, pltpu.SMEM)


def kernels_body(
    list_hbm, count_hbm, depth_hbm, amp_hbm, phase_hbm, out_ref,
    chosen_list, count, depth, amp, phase, table, screen, halves, made, small_sems, bulk_sems,
):
    screens, size, _ = amp.shape
    planes = depth.shape[0]
    kernel_size = out_ref.shape[1]
    small = [
        pltpu.make_async_copy(depth_hbm, depth, small_sems.at[0]),
        pltpu.make_async_copy(list_hbm, chosen_list, small_sems.at[1]),
        pltpu.make_async_copy(count_hbm, count, small_sems.at[2]),
    ]
    for copy in small:
        copy.start()

    def bulk(s):
        return [
            pltpu.make_async_copy(amp_hbm.at[s], amp.at[s], bulk_sems.at[0, s]),
            pltpu.make_async_copy(phase_hbm.at[s], phase.at[s], bulk_sems.at[1, s]),
        ]

    for copy in bulk(0):
        copy.start()

    frequency = lax.broadcasted_iota(jnp.int32, (kernel_size, size), 0) - kernel_size // 2
    cells = lax.broadcasted_iota(jnp.int32, (kernel_size, size), 1)
    turns = frequency.astype(jnp.float32) * cells.astype(jnp.float32) / size
    real_f, imag_f = cos_sin((2.0 * math.pi) * (turns - jnp.round(turns)))
    real_f = real_f.astype(jnp.bfloat16).astype(jnp.float32)
    imag_f = (-imag_f).astype(jnp.bfloat16).astype(jnp.float32)
    place = (lax.broadcasted_iota(jnp.int32, (1, size), 1).astype(jnp.float32) - size // 2) / size
    square = place * place
    for copy in small:
        copy.wait()
    for s in range(1, screens):
        for copy in bulk(s):
            copy.start()
    for p in range(planes):
        turns = depth[p] * square
        real_e, imag_e = cos_sin((2.0 * math.pi) * (turns - jnp.round(turns)))
        real_g = (real_f * real_e - imag_f * imag_e).astype(jnp.bfloat16)
        imag_g = (real_f * imag_e + imag_f * real_e).astype(jnp.bfloat16)
        top = slice(p * 2 * kernel_size, (p * 2 + 1) * kernel_size)
        low = slice((p * 2 + 1) * kernel_size, (p * 2 + 2) * kernel_size)
        table[top, :size] = real_g
        table[top, size:] = -imag_g
        table[low, :size] = imag_g
        table[low, size:] = real_g

    @pl.loop(0, screens)
    def _(s):
        for copy in bulk(s):
            copy.wait()
        magnitude = amp[s].astype(jnp.float32)
        real_e, imag_e = cos_sin(phase[s].astype(jnp.float32))
        screen[:size, :] = (magnitude * real_e).astype(jnp.bfloat16)
        screen[size:, :] = (magnitude * imag_e).astype(jnp.bfloat16)
        product = jnp.dot(table[...], screen[...], preferred_element_type=jnp.float32).astype(jnp.bfloat16)
        for p in range(planes):
            base = p * 2 * kernel_size
            halves[s, p, :, :size] = product[base : base + kernel_size]
            halves[s, p, :, size:] = product[base + kernel_size : base + 2 * kernel_size]

    for p in range(planes):
        second = lax.dot_general(
            jnp.concatenate([halves[s, p] for s in range(screens)], axis=0),
            table[p * 2 * kernel_size : (p + 1) * 2 * kernel_size, :],
            (((1,), (1,)), ((), ())),
            preferred_element_type=jnp.float32,
        )
        second = (second * (1.0 / size)).astype(jnp.bfloat16)
        for s in range(screens):
            made[s * planes + p] = second[s * kernel_size : (s + 1) * kernel_size]

    capacity, tiles = chosen_list.shape

    @pl.loop(0, tiles)
    def _(t):
        for c in range(capacity):
            chosen = made[chosen_list[c, t]]
            out_ref[t * capacity + c] = jnp.where(c < count[0, t], chosen, jnp.zeros_like(chosen))


def make_kernels(aperture_amp, aperture_phase, plane_depths, chosen_list, counts, kernel_size):
    screens, size, _ = aperture_amp.shape
    planes = plane_depths.shape[0]
    capacity, tiles = chosen_list.shape
    hbm = pl.BlockSpec(memory_space=pl.ANY)
    return pl.pallas_call(
        kernels_body,
        in_specs=[hbm] * 5,
        out_specs=pl.BlockSpec(memory_space=pltpu.VMEM),
        out_shape=pltpu.VMEM((tiles * capacity, kernel_size, 2 * kernel_size), jnp.bfloat16),
        scratch_shapes=[
            pltpu.SMEM((capacity, tiles), jnp.int32),
            pltpu.SMEM((1, tiles), jnp.int32),
            pltpu.SMEM((planes,), jnp.float32),
            pltpu.VMEM((screens, size, size), jnp.bfloat16),
            pltpu.VMEM((screens, size, size), jnp.bfloat16),
            pltpu.VMEM((planes * 2 * kernel_size, 2 * size), jnp.bfloat16),
            pltpu.VMEM((2 * size, size), jnp.bfloat16),
            pltpu.VMEM((screens, planes, kernel_size, 2 * size), jnp.bfloat16),
            pltpu.VMEM((screens * planes, kernel_size, 2 * kernel_size), jnp.bfloat16),
            pltpu.SemaphoreType.DMA((3,)),
            pltpu.SemaphoreType.DMA((2, screens)),
        ],
        compiler_params=pltpu.CompilerParams(vmem_limit_bytes=32 * 2**20),
        name="make_kernels",
    )(*map(in_hbm, (chosen_list, counts, plane_depths, aperture_amp, aperture_phase)))


class Layout:
    def __init__(self, blocks, anchors):
        self.parts = 3
        quads = (blocks + (QUAD - 1) * anchors) // QUAD + 1
        self.quads = (quads + STEP - 1) // STEP * STEP
        self.anchor = self.parts + 1
        self.slot = self.anchor + self.quads
        self.total = self.slot + (self.quads + UNROLL) * QUAD


def plan_body(
    pos_ref, slot_ref, count_ref, left_hbm, right_hbm, plan_ref, left_out, right_out,
    left_ref, right_ref, tally, cursor, sems, *, layout, row_slots, col_slots,
):
    anchors = row_slots * col_slots
    border = row_slots + col_slots - 1
    live = count_ref[0]

    def copies(block, place):
        return [
            pltpu.make_async_copy(left_hbm.at[block], left_ref.at[place], sems.at[0]),
            pltpu.make_async_copy(right_hbm.at[block], right_ref.at[place], sems.at[1]),
        ]

    def put(block, place, slot):
        plan_ref[layout.slot + place] = slot
        for copy in copies(block, place):
            copy.start()

    @pl.loop(0, anchors)
    def _(q):
        tally[q] = 0

    @pl.loop(0, live)
    def _(j):
        q = pos_ref[j]
        tally[q] = tally[q] + 1

    def lay(rank, quad):
        inner = rank - border
        q = jnp.where(
            rank < row_slots,
            rank * col_slots + col_slots - 1,
            jnp.where(
                rank < border,
                (row_slots - 1) * col_slots + rank - row_slots,
                (inner // (col_slots - 1)) * col_slots + lax.rem(inner, col_slots - 1),
            ),
        )
        number = tally[q]
        quads = (number + QUAD - 1) // QUAD
        cursor[q] = quad * QUAD

        @pl.loop(0, quads)
        def _(i):
            plan_ref[layout.anchor + quad + i] = q

        @pl.loop(quad * QUAD + number, (quad + quads) * QUAD)
        def _(i):
            put(0, i, -1)

        return quad + quads

    quad = 0
    begin = 0
    plan_ref[0] = 0
    for part, end in enumerate([row_slots, border, anchors]):
        quad = lax.fori_loop(begin, end, lay, quad)
        begin = end
        plan_ref[part + 1] = ((quad + STEP - 1) // STEP) * STEP

    full = ((quad + STEP - 1) // STEP) * STEP

    @pl.loop(quad, full)
    def _(i):
        plan_ref[layout.anchor + i] = 0
        for e in range(QUAD):
            put(0, i * QUAD + e, -1)

    quad = full

    @pl.loop(quad * QUAD, (quad + UNROLL) * QUAD)
    def _(i):
        plan_ref[layout.slot + i] = -1

    @pl.loop(0, live)
    def _(j):
        q = pos_ref[j]
        at = cursor[q]
        cursor[q] = at + 1
        put(j, at, slot_ref[j])

    chunk = STEP * QUAD

    @pl.loop(0, quad // STEP)
    def _(i):
        rows = pl.ds(0, chunk)
        pltpu.make_async_copy(left_hbm.at[rows], left_ref.at[rows], sems.at[0]).wait()
        pltpu.make_async_copy(right_hbm.at[rows], right_ref.at[rows], sems.at[1]).wait()

    def writes(i):
        rows = pl.ds(i * chunk, chunk)
        return [
            pltpu.make_async_copy(left_ref.at[rows], left_out.at[rows], sems.at[2]),
            pltpu.make_async_copy(right_ref.at[rows], right_out.at[rows], sems.at[3]),
        ]

    @pl.loop(0, quad // STEP)
    def _(i):
        for copy in writes(i):
            copy.start()

    @pl.loop(0, quad // STEP)
    def _(i):
        for copy in writes(i):
            copy.wait()


def plan_blocks(block_pos, block_slot, block_count, vis_left, vis_right, layout):
    kernel_size = vis_right.shape[1]
    row_slots, col_slots = TILE_U // kernel_size, TILE_V // kernel_size
    smem = pl.BlockSpec(memory_space=pltpu.SMEM)
    hbm = pl.BlockSpec(memory_space=pl.ANY)
    places = layout.quads * QUAD
    return pl.pallas_call(
        functools.partial(plan_body, layout=layout, row_slots=row_slots, col_slots=col_slots),
        in_specs=[smem] * 3 + [hbm] * 2,
        out_specs=[smem, hbm, hbm],
        out_shape=[
            pltpu.SMEM((layout.total,), jnp.int32),
            pltpu.HBM((places,) + vis_left.shape[1:], vis_left.dtype),
            pltpu.HBM((places,) + vis_right.shape[1:], vis_right.dtype),
        ],
        scratch_shapes=[
            pltpu.VMEM((places,) + vis_left.shape[1:], vis_left.dtype),
            pltpu.VMEM((places,) + vis_right.shape[1:], vis_right.dtype),
            pltpu.SMEM((row_slots * col_slots,), jnp.int32),
            pltpu.SMEM((row_slots * col_slots,), jnp.int32),
            pltpu.SemaphoreType.DMA((4,)),
        ],
        compiler_params=pltpu.CompilerParams(vmem_limit_bytes=36 * 2**20),
        name="plan_blocks",
    )(block_pos, block_slot, block_count, in_hbm(vis_left), in_hbm(vis_right))


def strip(sums, row_slots, col_slots, kernel_size, plane, a, col):
    patch = sums.shape[1]
    lanes = slice(plane * patch, (plane + 1) * patch)
    total = None
    if a < row_slots:
        total = sums[a * col_slots + col, :kernel_size, lanes]
    if a > 0:
        above = sums[(a - 1) * col_slots + col, kernel_size:, lanes]
        total = above if total is None else total + above
    return total


def grid_body(
    plan_ref, kern_ref, left_hbm, right_hbm, *rest, part, first_part, layout, row_slots, col_slots
):
    if not first_part:
        rest = rest[4:]
    sums, left_ring, right_ring, ahead, *rest = rest
    if first_part:
        col_ref, *rest = rest
    behind_ref, sems = rest
    mixed = (ahead, behind_ref)
    slots, kernel_size, _ = kern_ref.shape
    patch = left_hbm.shape[1]
    chunk = STEP * QUAD
    begin = plan_ref[part] // STEP
    end = plan_ref[part + 1] // STEP
    limit = jnp.minimum(plan_ref[layout.parts] // STEP, end + 2)

    def fetch(i):
        source = pl.ds(i * chunk, chunk)
        ring = lax.rem(i, RING)
        return [
            pltpu.make_async_copy(left_hbm.at[source], left_ring.at[ring], sems.at[0, ring]),
            pltpu.make_async_copy(right_hbm.at[source], right_ring.at[ring], sems.at[1, ring]),
        ]

    def start(i):
        @pl.when(i < limit)
        def _():
            for copy in reversed(fetch(i)):
                copy.start()

    def wait_new(i):
        if first_part:
            wait(i)
        else:
            pl.when(i > begin + 1)(lambda: wait(i))

    def wait(i):
        @pl.when(i < limit)
        def _():
            for copy in fetch(i):
                copy.wait()

    if first_part:
        start(0)

        @pl.loop(0, sums.shape[0])
        def _(q):
            sums[q] = jnp.zeros(sums.shape[1:], sums.dtype)

    zero = jnp.zeros((kernel_size, patch), jnp.bfloat16)

    def first(i, ring, at, ref, u):
        for e in range(QUAD):
            slot = plan_ref[layout.slot + (i * STEP + at) * QUAD + e]
            right = right_ring[ring, at * QUAD + e]
            kern = kern_ref[jnp.maximum(slot, 0)]
            kern = jnp.where(slot >= 0, kern, jnp.zeros_like(kern))
            spread = jnp.concatenate(
                [jnp.concatenate([right, zero], axis=1), jnp.concatenate([zero, right], axis=1)], axis=0
            )
            out = jnp.dot(kern, spread, preferred_element_type=jnp.float32).astype(jnp.bfloat16)
            top = slice(e * 2 * kernel_size, (e * 2 + 1) * kernel_size)
            low = slice((e * 2 + 1) * kernel_size, (e * 2 + 2) * kernel_size)
            ref[u, top, :] = out
            ref[u, low, :patch] = -out[:, patch:]
            ref[u, low, patch:] = out[:, :patch]

    def second(i, ring, at, ref, u):
        left = jnp.concatenate([left_ring[ring, at * QUAD + e] for e in range(QUAD)], axis=1)
        q = plan_ref[layout.anchor + i * STEP + at]
        sums[q] += jnp.dot(left, ref[u], preferred_element_type=jnp.float32)

    if first_part:
        fetch(0)[1].wait()
        start(1)
        for u in range(UNROLL):
            first(0, 0, u, mixed[0], u)
        fetch(0)[0].wait()
        start(2)
    else:
        start(begin + 2)

    @pl.loop(begin, end)
    def _(i):
        here = lax.rem(i, RING)
        there = lax.rem(i + 1, RING)
        start(i + 3)
        wait_new(i + 1)
        for u in range(UNROLL):
            first(i, here, UNROLL + u, mixed[1], u)
            second(i, here, u, mixed[0], u)
        for u in range(UNROLL):
            first(i + 1, there, u, mixed[0], u)
            second(i, here, UNROLL + u, mixed[1], u)

    wait_new(end + 1)
    if not first_part:
        return
    low = lax.broadcasted_iota(jnp.int32, (kernel_size, patch), 1) < kernel_size
    take = functools.partial(strip, sums, row_slots, col_slots, kernel_size)
    for a in range(row_slots + 1):
        real = pltpu.roll(take(0, a, col_slots - 1), kernel_size, 1)
        edge = jnp.where(low, real, take(1, a, col_slots - 1))
        col_ref[a * kernel_size : (a + 1) * kernel_size, :] = edge.astype(col_ref.dtype)


def row_body(before, col_ref, sums, row_ref, *, row_slots, col_slots):
    kernel_size = row_ref.shape[1]
    patch = sums.shape[1]
    low = lax.broadcasted_iota(jnp.int32, (kernel_size, patch), 1) < kernel_size
    take = functools.partial(strip, sums, row_slots, col_slots, kernel_size)
    corner = col_ref[row_slots * kernel_size :, :].astype(jnp.float32)
    for plane in range(2):
        behind = corner if plane == 0 else pltpu.roll(corner, kernel_size, 1)
        for tile in range(col_slots // 2):
            odd = pltpu.roll(take(plane, row_slots, 2 * tile + 1), kernel_size, 1)
            value = take(plane, row_slots, 2 * tile) + jnp.where(low, behind, odd)
            row_ref[plane, :, tile * patch : (tile + 1) * patch] = value.astype(row_ref.dtype)
            behind = odd


def row_halo(sums, col, kernel_size):
    vmem = pl.BlockSpec(memory_space=pltpu.VMEM)
    return pl.pallas_call(
        functools.partial(row_body, row_slots=TILE_U // kernel_size, col_slots=TILE_V // kernel_size),
        in_specs=[vmem] * 2,
        out_specs=[vmem] * 2,
        out_shape=[
            pltpu.VMEM(sums.shape, sums.dtype),
            pltpu.VMEM((2, kernel_size, TILE_V), jnp.bfloat16),
        ],
        input_output_aliases={0: 0},
        compiler_params=pltpu.CompilerParams(vmem_limit_bytes=4 * 2**20),
        name="row_halo",
    )(in_vmem(sums), in_vmem(col))


def grid_part(plan, part, kernels, left, right, carried, layout):
    kernel_size = kernels.shape[1]
    patch = left.shape[1]
    row_slots, col_slots = TILE_U // kernel_size, TILE_V // kernel_size
    smem = pl.BlockSpec(memory_space=pltpu.SMEM)
    vmem = pl.BlockSpec(memory_space=pltpu.VMEM)
    hbm = pl.BlockSpec(memory_space=pl.ANY)
    first_part = carried is None
    carried = [] if first_part else [in_vmem(array) for array in carried]
    mixed_shape = (UNROLL, QUAD * 2 * kernel_size, 2 * patch)
    out_shape = [
        pltpu.VMEM((row_slots * col_slots, patch, 2 * patch), jnp.float32),
        pltpu.VMEM((RING, STEP * QUAD) + left.shape[1:], left.dtype),
        pltpu.VMEM((RING, STEP * QUAD) + right.shape[1:], right.dtype),
        pltpu.VMEM(mixed_shape, jnp.bfloat16),
    ]
    if first_part:
        out_shape.append(pltpu.VMEM((TILE_U + kernel_size, 2 * kernel_size), jnp.bfloat16))
    out = pl.pallas_call(
        functools.partial(
            grid_body,
            part=part,
            first_part=first_part,
            layout=layout,
            row_slots=row_slots,
            col_slots=col_slots,
        ),
        in_specs=[smem, vmem, hbm, hbm] + [vmem] * len(carried),
        out_specs=[vmem] * len(out_shape),
        out_shape=out_shape,
        input_output_aliases={4 + i: i for i in range(len(carried))},
        scratch_shapes=[
            pltpu.VMEM(mixed_shape, jnp.bfloat16),
            pltpu.SemaphoreType.DMA((2, RING)),
        ],
        compiler_params=pltpu.CompilerParams(vmem_limit_bytes=12 * 2**20),
        name="grid_part",
    )(in_smem(plan), in_vmem(kernels), in_hbm(left), in_hbm(right), *carried)
    return out[:4], out[4:]


def merge_body(sums, row_ref, col_ref, out_hbm, out_ref, sems):
    kernel_size = row_ref.shape[1]
    patch = sums.shape[1]
    row_slots = out_ref.shape[1] // kernel_size
    col_slots = out_ref.shape[2] // kernel_size
    low = lax.broadcasted_iota(jnp.int32, (kernel_size, patch), 1) < kernel_size
    take = functools.partial(strip, sums, row_slots, col_slots, kernel_size)
    for a in range(row_slots):
        rows = slice(a * kernel_size, (a + 1) * kernel_size)
        edge = col_ref[rows, :].astype(jnp.float32)
        for plane in range(2):
            behind = edge if plane == 0 else pltpu.roll(edge, kernel_size, 1)
            for tile in range(col_slots // 2):
                lanes = slice(tile * patch, (tile + 1) * patch)
                odd = pltpu.roll(take(plane, a, 2 * tile + 1), kernel_size, 1)
                value = take(plane, a, 2 * tile) + jnp.where(low, behind, odd)
                if a == 0:
                    value = value + row_ref[plane, :, lanes].astype(jnp.float32)
                out_ref[plane, rows, lanes] = value
                behind = odd
        pltpu.make_async_copy(out_ref.at[:, rows], out_hbm.at[:, rows], sems.at[a]).start()
    for a in range(row_slots):
        rows = slice(a * kernel_size, (a + 1) * kernel_size)
        pltpu.make_async_copy(out_ref.at[:, rows], out_hbm.at[:, rows], sems.at[a]).wait()


def merge_tile(sums, row, col):
    vmem = pl.BlockSpec(memory_space=pltpu.VMEM)
    return pl.pallas_call(
        merge_body,
        in_specs=[vmem] * 3,
        out_specs=pl.BlockSpec(memory_space=pl.ANY),
        out_shape=jax.ShapeDtypeStruct((2, TILE_U, TILE_V), jnp.float32),
        scratch_shapes=[
            pltpu.VMEM((2, TILE_U, TILE_V), jnp.float32),
            pltpu.SemaphoreType.DMA((TILE_U // row.shape[1],)),
        ],
        compiler_params=pltpu.CompilerParams(vmem_limit_bytes=8 * 2**20),
        name="merge_tile",
    )(*map(in_vmem, (sums, row, col)))


def shards(
    aperture_amp,
    aperture_phase,
    plane_depths,
    send_list,
    send_count,
    vis_left,
    vis_right,
    block_slot,
    block_pos,
    block_count,
):
    kernel_size = vis_right.shape[1]
    tiles, capacity = send_list.shape[1:]
    both = ("tu", "tv")
    outgoing = make_kernels(
        aperture_amp, aperture_phase, plane_depths, send_list[0].T, send_count, kernel_size
    )
    outgoing = outgoing.reshape((tiles, capacity) + outgoing.shape[1:])
    arrived = lax.all_to_all(outgoing, both, split_axis=0, concat_axis=0, tiled=True)
    received = arrived.reshape((-1,) + arrived.shape[2:])
    layout = Layout(block_pos.shape[0], (TILE_U // kernel_size) * (TILE_V // kernel_size))
    plan, left, right = plan_blocks(block_pos, block_slot, block_count, vis_left, vis_right, layout)
    carried, (col,) = grid_part(plan, 0, received, left, right, None, layout)
    col = from_behind(col, "tv", 1)
    carried, _ = grid_part(plan, 1, received, left, right, carried, layout)
    sums, row = row_halo(carried[0], col, kernel_size)
    row = from_behind(row, "tu", 1)
    carried, _ = grid_part(plan, 2, received, left, right, [sums, *carried[1:]], layout)
    return merge_tile(carried[0], row, col)


def solution(mesh):
    placed = (
        P(("tu", "tv"), None, None),
        P(("tu", "tv"), None, None),
        P(),
        P(("tu", "tv"), None, None),
        P(("tu", "tv"), None),
        P(("tu", "tv"), None, None),
        P(("tu", "tv"), None, None),
        P(("tu", "tv")),
        P(("tu", "tv")),
        P(("tu", "tv")),
    )
    return jax.shard_map(
        shards, mesh=mesh, in_specs=placed, out_specs=P(None, "tu", "tv"), check_vma=False
    )
```

profile of v0, /device:TPU:1, one launch (start us, length us, event | category | flops | bytes accessed | tf_op | source)
XLA Modules:
  0.0 62.9 jit_solution(16419852462517645882)
XLA Ops:
  0.0 0.0 copy-start
  0.0 0.0 copy-start.1
  0.0 8.7 %make_kernels.1 = bf16[64,64,128]{2,1,0:T(8,128)(2,1)} custom-call(s32[2,32]{1,0:T(2,128)} %bitcast.8, s32[1,32]{1,0:T(1,128)} %count_hbm.1, f32[4]{0:T(128)} %depth_hbm.1, bf16[4,512,512]{2,1,0:T(8,128)(2,1)} %amp_hbm.1, bf16[4,512,512]{2,1,0:T(8,128)(2,1)} %phase_hbm.1), custom_call_target="tpu_custom_call" | custom-call | tf_op jit(solution)/shard_map/make_kernels/pallas_call | solution.py:148
  8.7 7.1 %all-to-all-start = ((bf16[32,2,64,128]{3,2,1,0:T(8,128)(2,1)}), bf16[32,2,64,128]{3,2,1,0:T(8,128)(2,1)S(1)}, u32[]{:S(2)}, u32[]{:S(2)}) async-start(bf16[32,2,64,128]{3,2,1,0:T(8,128)(2,1)} %bitcast.2), calls=%async_computation | async-start | bytes 2097152 | tf_op jit(solution)/shard_map/all_to_all | solution.py:568
  16.5 0.0 copy-done
  16.5 0.0 copy-done.1
  16.5 19.2 %plan_blocks.1 = (s32[660]{0:T(1024)S(4)}, bf16[512,128,128]{2,1,0:T(8,128)(2,1)}, bf16[512,64,128]{2,1,0:T(8,128)(2,1)}) custom-call(s32[384]{0:T(512)S(1)} %copy-done, s32[384]{0:T(512)S(1)} %copy-done.1, s32[1]{0:T(128)S(6)} %copy.29.count_ref, bf16[384,128,128]{2,1,0:T(8,128)(2,1)} %left_hbm.1, bf16[384,64,128]{2,1,0:T(8,128)(2,1)} %right_hbm.1), custom_call_target="tpu_custom_call" | custom-call | tf_op jit(solution)/shard_map/plan_blocks/pallas_call | solution.py:295
  35.7 5.5 %all-to-all-done = bf16[32,2,64,128]{3,2,1,0:T(8,128)(2,1)S(1)} async-done(((bf16[32,2,64,128]{3,2,1,0:T(8,128)(2,1)}), bf16[32,2,64,128]{3,2,1,0:T(8,128)(2,1)S(1)}, u32[]{:S(2)}, u32[]{:S(2)}) %all-to-all-start) | async-done | bytes 1048608 | tf_op jit(solution)/shard_map/all_to_all | solution.py:568
  41.2 4.2 %grid_part.3 = (f32[32,128,256]{2,1,0:T(8,128)S(1)}, bf16[4,32,128,128]{3,2,1,0:T(8,128)(2,1)S(1)}, bf16[4,32,64,128]{3,2,1,0:T(8,128)(2,1)S(1)}, bf16[4,512,256]{2,1,0:T(8,128)(2,1)S(1)}, bf16[320,128]{1,0:T(8,128)(2,1)S(1)}) custom-call(s32[660]{0:T(1024)S(4)} %get-tuple-element.20.plan_ref, bf16[64,64,128]{2,1,0:T(8,128)(2,1)S(1)} %bitcast.5, ...), custom_call_target="tpu_custom_call" | custom-call | tf_op jit(solution)/shard_map/grid_part/pallas_call | solution.py:484
  45.3 3.4 %collective-permute-start = (bf16[320,128]{1,0:T(8,128)(2,1)S(1)}, bf16[320,128]{1,0:T(8,128)(2,1)S(1)}, u32[]{:S(2)}, u32[]{:S(2)}) collective-permute-start(bf16[320,128]{1,0:T(8,128)(2,1)S(1)} %get-tuple-element.28), channel_id=1, source_target_pairs={{0,1},{1,2},{2,3},{4,5},{5,6},{6,7},{8,9},{9,10},{10,11},{12,13},{... | collective-permute-start | bytes 245768 | tf_op jit(solution)/shard_map/ppermute | solution.py:45
  48.8 3.0 %grid_part.4 = (f32[32,128,256]{2,1,0:T(8,128)S(1)}, bf16[4,32,128,128]{3,2,1,0:T(8,128)(2,1)S(1)}, bf16[4,32,64,128]{3,2,1,0:T(8,128)(2,1)S(1)}, bf16[4,512,256]{2,1,0:T(8,128)(2,1)S(1)}) custom-call(s32[660]{0:T(1024)S(4)} %get-tuple-element.20.plan_ref, ...), custom_call_target="tpu_custom_call", output_to_operand_aliasing={{0}: (4, {}), {1}: (5, {}), {2}: (6, {}), {3}: (7, {})} | custom-call | tf_op jit(solution)/shard_map/grid_part/pallas_call | solution.py:484
  51.8 0.0 collective-permute-done.col_ref
  51.8 0.1 row_halo.1
  51.9 3.1 %collective-permute-start.1 = (bf16[2,64,512]{2,1,0:T(8,128)(2,1)S(1)}, bf16[2,64,512]{2,1,0:T(8,128)(2,1)S(1)}, u32[]{:S(2)}, u32[]{:S(2)}) collective-permute-start(bf16[2,64,512]{2,1,0:T(8,128)(2,1)S(1)} %get-tuple-element.34), channel_id=1, source_target_pairs={{0,4},{4,8},{8,12},{12,16},{16,20},{20,24},{24,28},{1,5},{5,9},{9,... | collective-permute-start | bytes 393224 | tf_op jit(solution)/shard_map/ppermute | solution.py:45
  55.0 6.7 %grid_part.5 = (f32[32,128,256]{2,1,0:T(8,128)S(1)}, bf16[4,32,128,128]{3,2,1,0:T(8,128)(2,1)S(1)}, bf16[4,32,64,128]{3,2,1,0:T(8,128)(2,1)S(1)}, bf16[4,512,256]{2,1,0:T(8,128)(2,1)S(1)}) custom-call(s32[660]{0:T(1024)S(4)} %get-tuple-element.20.plan_ref, ...), custom_call_target="tpu_custom_call", output_to_operand_aliasing={{0}: (4, {}), {1}: (5, {}), {2}: (6, {}), {3}: (7, {})} | custom-call | tf_op jit(solution)/shard_map/grid_part/pallas_call | solution.py:484
  61.8 0.0 collective-permute-done.1.row_ref
  61.8 1.1 %merge_tile.1 = f32[2,256,512]{2,1,0:T(8,128)} custom-call(f32[32,128,256]{2,1,0:T(8,128)S(1)} %get-tuple-element.33.sums, bf16[2,64,512]{2,1,0:T(8,128)(2,1)S(1)} %collective-permute-done.1.row_ref, bf16[320,128]{1,0:T(8,128)(2,1)S(1)} %collective-permute-done.col_ref), custom_call_target="tpu_custom_call" | custom-call | tf_op jit(solution)/shard_map/merge_tile/pallas_call | solution.py:535
Async XLA Ops:
  0.0 16.5 %copy-start = (s32[384]{0:T(512)S(1)}, s32[384]{0:T(512)}, u32[]{:S(2)}) copy-start(s32[384]{0:T(512)} %pos_ref.1) | copy-start | bytes 4612
  0.0 16.5 %copy-start.1 = (s32[384]{0:T(512)S(1)}, s32[384]{0:T(512)}, u32[]{:S(2)}) copy-start(s32[384]{0:T(512)} %slot_ref.1) | copy-start | bytes 4612
  8.7 32.4 %all-to-all-start = ((bf16[32,2,64,128]{3,2,1,0:T(8,128)(2,1)}), bf16[32,2,64,128]{3,2,1,0:T(8,128)(2,1)S(1)}, u32[]{:S(2)}, u32[]{:S(2)}) async-start(bf16[32,2,64,128]{3,2,1,0:T(8,128)(2,1)} %bitcast.2), calls=%async_computation | async-start | bytes 2097152 | tf_op jit(solution)/shard_map/all_to_all | solution.py:568
  45.3 6.4 %collective-permute-start = (bf16[320,128]{1,0:T(8,128)(2,1)S(1)}, bf16[320,128]{1,0:T(8,128)(2,1)S(1)}, u32[]{:S(2)}, u32[]{:S(2)}) collective-permute-start(bf16[320,128]{1,0:T(8,128)(2,1)S(1)} %get-tuple-element.28), channel_id=1, source_target_pairs={{0,1},{1,2},{2,3},{4,5},{5,6},{6,7},{8,9},{9,10},{10,11},{12,13},{... | collective-permute-start | bytes 245768 | tf_op jit(solution)/shard_map/ppermute | solution.py:45
  51.9 9.9 %collective-permute-start.1 = (bf16[2,64,512]{2,1,0:T(8,128)(2,1)S(1)}, bf16[2,64,512]{2,1,0:T(8,128)(2,1)S(1)}, u32[]{:S(2)}, u32[]{:S(2)}) collective-permute-start(bf16[2,64,512]{2,1,0:T(8,128)(2,1)S(1)} %get-tuple-element.34), channel_id=1, source_target_pairs={{0,4},{4,8},{8,12},{12,16},{16,20},{20,24},{24,28},{1,5},{5,9},{9,... | collective-permute-start | bytes 393224 | tf_op jit(solution)/shard_map/ppermute | solution.py:45
where the time goes:
time: 62.3 us; the launch traced here: 62.9 us
  Pallas kernels  43.1 us (69%)
  starting transfers between devices  13.6 us (22%)
  waiting for transfers between devices  5.46 us (9%)
  between operations  0.75 us (1%)
    pallas_call x1, Pallas kernels, plan_blocks(): pl.pallas_call(functools.partial(plan_body, layout=layout, row_slots=row_...  19.2 us
    pallas_call x3, Pallas kernels, grid_part(): pl.pallas_call(functools.partial(grid_body, part=part, first_part=first_p...  13.9 us
    pallas_call x1, Pallas kernels, make_kernels(): pl.pallas_call(kernels_body, in_specs=[hbm] * 5, out_specs=pl.BlockSpec(m...  8.73 us
    all_to_all x1, starting transfers between devices, shards(): lax.all_to_all(outgoing, both, split_axis=0, concat_axis=0, tiled=True)  7.1 us
    ppermute x2, starting transfers between devices, from_behind(): return lax.ppermute(block, axis, route)  6.51 us
    all_to_all x1, waiting for transfers between devices, shards(): lax.all_to_all(outgoing, both, split_axis=0, concat_axis=0, tiled=True)  5.45 us
  transfers between devices with their start and end apart: 3, of which 1 were waited for; matrix products, arithmetic and copies ran while one was open for 0% of the time, Pallas kernels for 46%

commit v1 on v0

--- a/solution.py
+++ b/solution.py
@@ -15,6 +15,7 @@
 UNROLL = 4
 STEP = 2 * UNROLL
 RING = 4
+LEFT, RIGHT = 0, 1
 
 def _fit(fn, degree):
     span = math.pi ** 2
@@ -350,26 +351,22 @@
             pltpu.make_async_copy(right_hbm.at[source], right_ring.at[ring], sems.at[1, ring]),
         ]
 
-    def start(i):
+    def start(i, which):
         @pl.when(i < limit)
         def _():
-            for copy in reversed(fetch(i)):
-                copy.start()
-
-    def wait_new(i):
-        if first_part:
-            wait(i)
-        else:
-            pl.when(i > begin + 1)(lambda: wait(i))
-
-    def wait(i):
-        @pl.when(i < limit)
+            fetch(i)[which].start()
+
+    def wait(i, which):
+        fresh = (i < limit) if first_part else ((i < limit) & (i > begin + 1))
+
+        @pl.when(fresh)
         def _():
-            for copy in fetch(i):
-                copy.wait()
+            fetch(i)[which].wait()
 
     if first_part:
-        start(0)
+        start(0, RIGHT)
+        start(1, RIGHT)
+        start(0, LEFT)
 
         @pl.loop(0, sums.shape[0])
         def _(q):
@@ -399,21 +396,21 @@
         sums[q] += jnp.dot(left, ref[u], preferred_element_type=jnp.float32)
 
     if first_part:
-        fetch(0)[1].wait()
-        start(1)
+        wait(0, RIGHT)
+        start(1, LEFT)
         for u in range(UNROLL):
             first(0, 0, u, mixed[0], u)
-        fetch(0)[0].wait()
-        start(2)
-    else:
-        start(begin + 2)
+    start(begin + 2, RIGHT)
+    start(begin + 2, LEFT)
 
     @pl.loop(begin, end)
     def _(i):
         here = lax.rem(i, RING)
         there = lax.rem(i + 1, RING)
-        start(i + 3)
-        wait_new(i + 1)
+        start(i + 3, RIGHT)
+        start(i + 3, LEFT)
+        wait(i, LEFT)
+        wait(i + 1, RIGHT)
         for u in range(UNROLL):
             first(i, here, UNROLL + u, mixed[1], u)
             second(i, here, u, mixed[0], u)
@@ -421,7 +418,9 @@
             first(i + 1, there, u, mixed[0], u)
             second(i, here, UNROLL + u, mixed[1], u)
 
-    wait_new(end + 1)
+    wait(end, LEFT)
+    wait(end + 1, LEFT)
+    wait(end + 1, RIGHT)
     if not first_part:
         return
     low = lax.broadcasted_iota(jnp.int32, (kernel_size, patch), 1) < kernel_size

time: 62.3 us -> 62.7 us (level)
  starting transfers between devices: 13.6 us -> 15.1 us
  Pallas kernels: 43.1 us -> 42.1 us
    ppermute x2, starting transfers between devices: 6.51 us -> 7.95 us  [from_behind(): return lax.ppermute(block, axis, route)]
    pallas_call x3, Pallas kernels: 13.9 us -> 12.7 us  [grid_part(): pl.pallas_call(functools.partial(grid_body, part=part, first_part=first_p...]
  transfers between devices with their start and end apart: 3 -> 3, of which waited for: 1 -> 1; matrix products, arithmetic and copies ran while one was open for 0% -> 0% of each run, Pallas kernels for 46% -> 45%
where the time goes in v1:
time: 62.7 us; the launch traced here: 63.2 us
  Pallas kernels  42.1 us (67%)
  starting transfers between devices  15.1 us (24%)
  waiting for transfers between devices  5.3 us (8%)
  between operations  0.75 us (1%)
    pallas_call x1, Pallas kernels, plan_blocks(): pl.pallas_call(functools.partial(plan_body, layout=layout, row_slots=row_...  19.4 us
    pallas_call x3, Pallas kernels, grid_part(): pl.pallas_call(functools.partial(grid_body, part=part, first_part=first_p...  12.7 us
    pallas_call x1, Pallas kernels, make_kernels(): pl.pallas_call(kernels_body, in_specs=[hbm] * 5, out_specs=pl.BlockSpec(m...  8.73 us
    ppermute x2, starting transfers between devices, from_behind(): return lax.ppermute(block, axis, route)  7.95 us
    all_to_all x1, starting transfers between devices, shards(): lax.all_to_all(outgoing, both, split_axis=0, concat_axis=0, tiled=True)  7.1 us
    all_to_all x1, waiting for transfers between devices, shards(): lax.all_to_all(outgoing, both, split_axis=0, concat_axis=0, tiled=True)  5.29 us
  transfers between devices with their start and end apart: 3, of which 1 were waited for; matrix products, arithmetic and copies ran while one was open for 0% of the time, Pallas kernels for 45%

profile of v1, /device:TPU:1, one launch (start us, length us, event | category | flops | bytes accessed | tf_op | source)
XLA Modules:
  0.0 63.2 jit_solution(14451914396935014628)
XLA Ops:
  0.0 0.0 copy-start
  0.0 0.0 copy-start.1
  0.0 8.7 %make_kernels.1 = bf16[64,64,128]{2,1,0:T(8,128)(2,1)} custom-call(s32[2,32]{1,0:T(2,128)} %bitcast.8, s32[1,32]{1,0:T(1,128)} %count_hbm.1, f32[4]{0:T(128)} %depth_hbm.1, bf16[4,512,512]{2,1,0:T(8,128)(2,1)} %amp_hbm.1, bf16[4,512,512]{2,1,0:T(8,128)(2,1)} %phase_hbm.1), custom_call_target="tpu_custom_call" | custom-call | tf_op jit(solution)/shard_map/make_kernels/pallas_call | solution.py:149
  8.7 7.1 %all-to-all-start = ((bf16[32,2,64,128]{3,2,1,0:T(8,128)(2,1)}), bf16[32,2,64,128]{3,2,1,0:T(8,128)(2,1)S(1)}, u32[]{:S(2)}, u32[]{:S(2)}) async-start(bf16[32,2,64,128]{3,2,1,0:T(8,128)(2,1)} %bitcast.2), calls=%async_computation | async-start | bytes 2097152 | tf_op jit(solution)/shard_map/all_to_all | solution.py:567
  16.5 0.0 copy-done
  16.5 0.0 copy-done.1
  16.5 19.4 %plan_blocks.1 = (s32[660]{0:T(1024)S(4)}, bf16[512,128,128]{2,1,0:T(8,128)(2,1)}, bf16[512,64,128]{2,1,0:T(8,128)(2,1)}) custom-call(s32[384]{0:T(512)S(1)} %copy-done, s32[384]{0:T(512)S(1)} %copy-done.1, s32[1]{0:T(128)S(6)} %copy.29.count_ref, bf16[384,128,128]{2,1,0:T(8,128)(2,1)} %left_hbm.1, bf16[384,64,128]{2,1,0:T(8,128)(2,1)} %right_hbm.1), custom_call_target="tpu_custom_call" | custom-call | tf_op jit(solution)/shard_map/plan_blocks/pallas_call | solution.py:296
  35.9 5.3 %all-to-all-done = bf16[32,2,64,128]{3,2,1,0:T(8,128)(2,1)S(1)} async-done(((bf16[32,2,64,128]{3,2,1,0:T(8,128)(2,1)}), bf16[32,2,64,128]{3,2,1,0:T(8,128)(2,1)S(1)}, u32[]{:S(2)}, u32[]{:S(2)}) %all-to-all-start) | async-done | bytes 1048608 | tf_op jit(solution)/shard_map/all_to_all | solution.py:567
  41.2 3.6 %grid_part.3 = (f32[32,128,256]{2,1,0:T(8,128)S(1)}, bf16[4,32,128,128]{3,2,1,0:T(8,128)(2,1)S(1)}, bf16[4,32,64,128]{3,2,1,0:T(8,128)(2,1)S(1)}, bf16[4,512,256]{2,1,0:T(8,128)(2,1)S(1)}, bf16[320,128]{1,0:T(8,128)(2,1)S(1)}) custom-call(s32[660]{0:T(1024)S(4)} %get-tuple-element.20.plan_ref, bf16[64,64,128]{2,1,0:T(8,128)(2,1)S(1)} %bitcast.5, ...), custom_call_target="tpu_custom_call" | custom-call | tf_op jit(solution)/shard_map/grid_part/pallas_call | solution.py:483
  44.8 4.2 %collective-permute-start = (bf16[320,128]{1,0:T(8,128)(2,1)S(1)}, bf16[320,128]{1,0:T(8,128)(2,1)S(1)}, u32[]{:S(2)}, u32[]{:S(2)}) collective-permute-start(bf16[320,128]{1,0:T(8,128)(2,1)S(1)} %get-tuple-element.28), channel_id=1, source_target_pairs={{0,1},{1,2},{2,3},{4,5},{5,6},{6,7},{8,9},{9,10},{10,11},{12,13},{... | collective-permute-start | bytes 245768 | tf_op jit(solution)/shard_map/ppermute | solution.py:46
  48.9 2.0 %grid_part.4 = (f32[32,128,256]{2,1,0:T(8,128)S(1)}, bf16[4,32,128,128]{3,2,1,0:T(8,128)(2,1)S(1)}, bf16[4,32,64,128]{3,2,1,0:T(8,128)(2,1)S(1)}, bf16[4,512,256]{2,1,0:T(8,128)(2,1)S(1)}) custom-call(s32[660]{0:T(1024)S(4)} %get-tuple-element.20.plan_ref, ...), custom_call_target="tpu_custom_call", output_to_operand_aliasing={{0}: (4, {}), {1}: (5, {}), {2}: (6, {}), {3}: (7, {})} | custom-call | tf_op jit(solution)/shard_map/grid_part/pallas_call | solution.py:483
  50.9 0.0 collective-permute-done.col_ref
  50.9 0.1 row_halo.1
  51.1 3.8 %collective-permute-start.1 = (bf16[2,64,512]{2,1,0:T(8,128)(2,1)S(1)}, bf16[2,64,512]{2,1,0:T(8,128)(2,1)S(1)}, u32[]{:S(2)}, u32[]{:S(2)}) collective-permute-start(bf16[2,64,512]{2,1,0:T(8,128)(2,1)S(1)} %get-tuple-element.34), channel_id=1, source_target_pairs={{0,4},{4,8},{8,12},{12,16},{16,20},{20,24},{24,28},{1,5},{5,9},{9,... | collective-permute-start | bytes 393224 | tf_op jit(solution)/shard_map/ppermute | solution.py:46
  54.9 7.2 %grid_part.5 = (f32[32,128,256]{2,1,0:T(8,128)S(1)}, bf16[4,32,128,128]{3,2,1,0:T(8,128)(2,1)S(1)}, bf16[4,32,64,128]{3,2,1,0:T(8,128)(2,1)S(1)}, bf16[4,512,256]{2,1,0:T(8,128)(2,1)S(1)}) custom-call(s32[660]{0:T(1024)S(4)} %get-tuple-element.20.plan_ref, ...), custom_call_target="tpu_custom_call", output_to_operand_aliasing={{0}: (4, {}), {1}: (5, {}), {2}: (6, {}), {3}: (7, {})} | custom-call | tf_op jit(solution)/shard_map/grid_part/pallas_call | solution.py:483
  62.0 0.0 collective-permute-done.1.row_ref
  62.0 1.1 %merge_tile.1 = f32[2,256,512]{2,1,0:T(8,128)} custom-call(f32[32,128,256]{2,1,0:T(8,128)S(1)} %get-tuple-element.33.sums, bf16[2,64,512]{2,1,0:T(8,128)(2,1)S(1)} %collective-permute-done.1.row_ref, bf16[320,128]{1,0:T(8,128)(2,1)S(1)} %collective-permute-done.col_ref), custom_call_target="tpu_custom_call" | custom-call | tf_op jit(solution)/shard_map/merge_tile/pallas_call | solution.py:534
Async XLA Ops:
  0.0 16.5 %copy-start = (s32[384]{0:T(512)S(1)}, s32[384]{0:T(512)}, u32[]{:S(2)}) copy-start(s32[384]{0:T(512)} %pos_ref.1) | copy-start | bytes 4612
  0.0 16.5 %copy-start.1 = (s32[384]{0:T(512)S(1)}, s32[384]{0:T(512)}, u32[]{:S(2)}) copy-start(s32[384]{0:T(512)} %slot_ref.1) | copy-start | bytes 4612
  8.7 32.4 %all-to-all-start = ((bf16[32,2,64,128]{3,2,1,0:T(8,128)(2,1)}), bf16[32,2,64,128]{3,2,1,0:T(8,128)(2,1)S(1)}, u32[]{:S(2)}, u32[]{:S(2)}) async-start(bf16[32,2,64,128]{3,2,1,0:T(8,128)(2,1)} %bitcast.2), calls=%async_computation | async-start | bytes 2097152 | tf_op jit(solution)/shard_map/all_to_all | solution.py:567
  44.8 6.1 %collective-permute-start = (bf16[320,128]{1,0:T(8,128)(2,1)S(1)}, bf16[320,128]{1,0:T(8,128)(2,1)S(1)}, u32[]{:S(2)}, u32[]{:S(2)}) collective-permute-start(bf16[320,128]{1,0:T(8,128)(2,1)S(1)} %get-tuple-element.28), channel_id=1, source_target_pairs={{0,1},{1,2},{2,3},{4,5},{5,6},{6,7},{8,9},{9,10},{10,11},{12,13},{... | collective-permute-start | bytes 245768 | tf_op jit(solution)/shard_map/ppermute | solution.py:46
  51.1 11.0 %collective-permute-start.1 = (bf16[2,64,512]{2,1,0:T(8,128)(2,1)S(1)}, bf16[2,64,512]{2,1,0:T(8,128)(2,1)S(1)}, u32[]{:S(2)}, u32[]{:S(2)}) collective-permute-start(bf16[2,64,512]{2,1,0:T(8,128)(2,1)S(1)} %get-tuple-element.34), channel_id=1, source_target_pairs={{0,4},{4,8},{8,12},{12,16},{16,20},{20,24},{24,28},{1,5},{5,9},{9,... | collective-permute-start | bytes 393224 | tf_op jit(solution)/shard_map/ppermute | solution.py:46

commit v2 on v1

--- a/solution.py
+++ b/solution.py
@@ -40,10 +40,13 @@
     return horner(COS_POLY, u), x * horner(SIN_POLY, u)
 
 
-def from_behind(block, axis, distance):
-    devices = range(lax.axis_size(axis))
-    route = [(i - distance, i) for i in devices if i - distance in devices]
-    return lax.ppermute(block, axis, route)
+def around(block, axis):
+    devices = lax.axis_size(axis)
+    return lax.ppermute(block, axis, [(i, (i + 1) % devices) for i in range(devices)])
+
+
+def past_first(axis, halo):
+    return jnp.where(lax.axis_index(axis) > 0, halo.astype(jnp.float32), 0.0)
 
 
 def in_hbm(array):
@@ -436,7 +439,7 @@
     patch = sums.shape[1]
     low = lax.broadcasted_iota(jnp.int32, (kernel_size, patch), 1) < kernel_size
     take = functools.partial(strip, sums, row_slots, col_slots, kernel_size)
-    corner = col_ref[row_slots * kernel_size :, :].astype(jnp.float32)
+    corner = past_first("tv", col_ref[row_slots * kernel_size :, :])
     for plane in range(2):
         behind = corner if plane == 0 else pltpu.roll(corner, kernel_size, 1)
         for tile in range(col_slots // 2):
@@ -512,7 +515,7 @@
     take = functools.partial(strip, sums, row_slots, col_slots, kernel_size)
     for a in range(row_slots):
         rows = slice(a * kernel_size, (a + 1) * kernel_size)
-        edge = col_ref[rows, :].astype(jnp.float32)
+        edge = past_first("tv", col_ref[rows, :])
         for plane in range(2):
             behind = edge if plane == 0 else pltpu.roll(edge, kernel_size, 1)
             for tile in range(col_slots // 2):
@@ -520,7 +523,7 @@
                 odd = pltpu.roll(take(plane, a, 2 * tile + 1), kernel_size, 1)
                 value = take(plane, a, 2 * tile) + jnp.where(low, behind, odd)
                 if a == 0:
-                    value = value + row_ref[plane, :, lanes].astype(jnp.float32)
+                    value = value + past_first("tu", row_ref[plane, :, lanes])
                 out_ref[plane, rows, lanes] = value
                 behind = odd
         pltpu.make_async_copy(out_ref.at[:, rows], out_hbm.at[:, rows], sems.at[a]).start()
@@ -569,10 +572,10 @@
     layout = Layout(block_pos.shape[0], (TILE_U // kernel_size) * (TILE_V // kernel_size))
     plan, left, right = plan_blocks(block_pos, block_slot, block_count, vis_left, vis_right, layout)
     carried, (col,) = grid_part(plan, 0, received, left, right, None, layout)
-    col = from_behind(col, "tv", 1)
+    col = around(col, "tv")
     carried, _ = grid_part(plan, 1, received, left, right, carried, layout)
     sums, row = row_halo(carried[0], col, kernel_size)
-    row = from_behind(row, "tu", 1)
+    row = around(row, "tu")
     carried, _ = grid_part(plan, 2, received, left, right, [sums, *carried[1:]], layout)
     return merge_tile(carried[0], row, col)
 

time: 62.7 us -> 59.1 us (0.943)
  the two profiles are of different devices: /device:TPU:1 before, /device:TPU:0 now
where the time goes in v2:
time: 59.1 us; the launch traced here: 58.4 us
  Pallas kernels  30 us (51%)
  waiting for transfers between devices  18.4 us (31%)
  starting transfers between devices  9.35 us (16%)
  between operations  0.73 us (1%)
    all_to_all x1, waiting for transfers between devices, shards(): lax.all_to_all(outgoing, both, split_axis=0, concat_axis=0, tiled=True)  13.5 us
    pallas_call x1, Pallas kernels, plan_blocks(): pl.pallas_call(functools.partial(plan_body, layout=layout, row_slots=row_...  12 us
    pallas_call x1, Pallas kernels, make_kernels(): pl.pallas_call(kernels_body, in_specs=[hbm] * 5, out_specs=pl.BlockSpec(m...  8.73 us
    pallas_call x3, Pallas kernels, grid_part(): pl.pallas_call(functools.partial(grid_body, part=part, first_part=first_p...  7.96 us
    all_to_all x1, starting transfers between devices, shards(): lax.all_to_all(outgoing, both, split_axis=0, concat_axis=0, tiled=True)  7.3 us
    ppermute x2, waiting for transfers between devices, around(): lax.ppermute(block, axis, [(i, (i + 1) % devices) for i in range(devices)])  4.83 us
    ppermute x2, starting transfers between devices, around(): lax.ppermute(block, axis, [(i, (i + 1) % devices) for i in range(devices)])  2.04 us
  transfers between devices with their start and end apart: 3, of which 3 were waited for; matrix products, arithmetic and copies ran while one was open for 0% of the time, Pallas kernels for 29%

profile of v2, /device:TPU:0, one launch (start us, length us, event | category | flops | bytes accessed | tf_op | source)
XLA Modules:
  0.0 58.4 jit_solution(6125615845790879269)
XLA Ops:
  0.0 0.0 copy-start
  0.0 0.0 copy-start.1
  0.0 8.7 %make_kernels.1 = bf16[64,64,128]{2,1,0:T(8,128)(2,1)} custom-call(s32[2,32]{1,0:T(2,128)} %bitcast.8, s32[1,32]{1,0:T(1,128)} %count_hbm.1, f32[4]{0:T(128)} %depth_hbm.1, bf16[4,512,512]{2,1,0:T(8,128)(2,1)} %amp_hbm.1, bf16[4,512,512]{2,1,0:T(8,128)(2,1)} %phase_hbm.1), custom_call_target="tpu_custom_call" | custom-call | tf_op jit(solution)/shard_map/make_kernels/pallas_call | solution.py:152
  8.7 7.3 %all-to-all-start = ((bf16[32,2,64,128]{3,2,1,0:T(8,128)(2,1)}), bf16[32,2,64,128]{3,2,1,0:T(8,128)(2,1)S(1)}, u32[]{:S(2)}, u32[]{:S(2)}) async-start(bf16[32,2,64,128]{3,2,1,0:T(8,128)(2,1)} %bitcast.2), calls=%async_computation | async-start | bytes 2097152 | tf_op jit(solution)/shard_map/all_to_all | solution.py:570
  16.7 0.0 copy-done
  16.7 0.0 copy-done.1
  16.7 12.0 %plan_blocks.1 = (s32[660]{0:T(1024)S(4)}, bf16[512,128,128]{2,1,0:T(8,128)(2,1)}, bf16[512,64,128]{2,1,0:T(8,128)(2,1)}) custom-call(s32[384]{0:T(512)S(1)} %copy-done, s32[384]{0:T(512)S(1)} %copy-done.1, s32[1]{0:T(128)S(6)} %copy.29.count_ref, bf16[384,128,128]{2,1,0:T(8,128)(2,1)} %left_hbm.1, bf16[384,64,128]{2,1,0:T(8,128)(2,1)} %right_hbm.1), custom_call_target="tpu_custom_call" | custom-call | tf_op jit(solution)/shard_map/plan_blocks/pallas_call | solution.py:299
  28.8 13.5 %all-to-all-done = bf16[32,2,64,128]{3,2,1,0:T(8,128)(2,1)S(1)} async-done(((bf16[32,2,64,128]{3,2,1,0:T(8,128)(2,1)}), bf16[32,2,64,128]{3,2,1,0:T(8,128)(2,1)S(1)}, u32[]{:S(2)}, u32[]{:S(2)}) %all-to-all-start) | async-done | bytes 1048608 | tf_op jit(solution)/shard_map/all_to_all | solution.py:570
  42.3 3.1 %grid_part.3 = (f32[32,128,256]{2,1,0:T(8,128)S(1)}, bf16[4,32,128,128]{3,2,1,0:T(8,128)(2,1)S(1)}, bf16[4,32,64,128]{3,2,1,0:T(8,128)(2,1)S(1)}, bf16[4,512,256]{2,1,0:T(8,128)(2,1)S(1)}, bf16[320,128]{1,0:T(8,128)(2,1)S(1)}) custom-call(s32[660]{0:T(1024)S(4)} %get-tuple-element.20.plan_ref, bf16[64,64,128]{2,1,0:T(8,128)(2,1)S(1)} %bitcast.5, ...), custom_call_target="tpu_custom_call" | custom-call | tf_op jit(solution)/shard_map/grid_part/pallas_call | solution.py:486
  45.4 0.1 collective-permute-start
  45.5 1.5 %grid_part.4 = (f32[32,128,256]{2,1,0:T(8,128)S(1)}, bf16[4,32,128,128]{3,2,1,0:T(8,128)(2,1)S(1)}, bf16[4,32,64,128]{3,2,1,0:T(8,128)(2,1)S(1)}, bf16[4,512,256]{2,1,0:T(8,128)(2,1)S(1)}) custom-call(s32[660]{0:T(1024)S(4)} %get-tuple-element.20.plan_ref, ...), custom_call_target="tpu_custom_call", output_to_operand_aliasing={{0}: (4, {}), {1}: (5, {}), {2}: (6, {}), {3}: (7, {})} | custom-call | tf_op jit(solution)/shard_map/grid_part/pallas_call | solution.py:486
  47.0 2.4 %collective-permute-done.col_ref = bf16[320,128]{1,0:T(8,128)(2,1)S(1)} collective-permute-done((bf16[320,128]{1,0:T(8,128)(2,1)S(1)}, bf16[320,128]{1,0:T(8,128)(2,1)S(1)}, u32[]{:S(2)}, u32[]{:S(2)}) %collective-permute-start) | collective-permute-done | bytes 81952 | tf_op jit(solution)/shard_map/ppermute | solution.py:45
  49.3 0.1 row_halo.1
  49.5 2.0 %collective-permute-start.1 = (bf16[2,64,512]{2,1,0:T(8,128)(2,1)S(1)}, bf16[2,64,512]{2,1,0:T(8,128)(2,1)S(1)}, u32[]{:S(2)}, u32[]{:S(2)}) collective-permute-start(bf16[2,64,512]{2,1,0:T(8,128)(2,1)S(1)} %get-tuple-element.34), channel_id=1, source_target_pairs={{0,4},{4,8},{8,12},{12,16},{16,20},{20,24},{24,28},{28,0},{1,5},{5... | collective-permute-start | bytes 393224 | tf_op jit(solution)/shard_map/ppermute | solution.py:45
  51.5 3.4 %grid_part.5 = (f32[32,128,256]{2,1,0:T(8,128)S(1)}, bf16[4,32,128,128]{3,2,1,0:T(8,128)(2,1)S(1)}, bf16[4,32,64,128]{3,2,1,0:T(8,128)(2,1)S(1)}, bf16[4,512,256]{2,1,0:T(8,128)(2,1)S(1)}) custom-call(s32[660]{0:T(1024)S(4)} %get-tuple-element.20.plan_ref, ...), custom_call_target="tpu_custom_call", output_to_operand_aliasing={{0}: (4, {}), {1}: (5, {}), {2}: (6, {}), {3}: (7, {})} | custom-call | tf_op jit(solution)/shard_map/grid_part/pallas_call | solution.py:486
  54.8 2.5 %collective-permute-done.1.row_ref = bf16[2,64,512]{2,1,0:T(8,128)(2,1)S(1)} collective-permute-done((bf16[2,64,512]{2,1,0:T(8,128)(2,1)S(1)}, bf16[2,64,512]{2,1,0:T(8,128)(2,1)S(1)}, u32[]{:S(2)}, u32[]{:S(2)}) %collective-permute-start.1) | collective-permute-done | bytes 131104 | tf_op jit(solution)/shard_map/ppermute | solution.py:45
  57.3 1.1 %merge_tile.1 = f32[2,256,512]{2,1,0:T(8,128)} custom-call(f32[32,128,256]{2,1,0:T(8,128)S(1)} %get-tuple-element.33.sums, bf16[2,64,512]{2,1,0:T(8,128)(2,1)S(1)} %collective-permute-done.1.row_ref, bf16[320,128]{1,0:T(8,128)(2,1)S(1)} %collective-permute-done.col_ref), custom_call_target="tpu_custom_call" | custom-call | tf_op jit(solution)/shard_map/merge_tile/pallas_call | solution.py:537
Async XLA Ops:
  0.0 16.7 %copy-start = (s32[384]{0:T(512)S(1)}, s32[384]{0:T(512)}, u32[]{:S(2)}) copy-start(s32[384]{0:T(512)} %pos_ref.1) | copy-start | bytes 4612
  0.0 16.7 %copy-start.1 = (s32[384]{0:T(512)S(1)}, s32[384]{0:T(512)}, u32[]{:S(2)}) copy-start(s32[384]{0:T(512)} %slot_ref.1) | copy-start | bytes 4612
  8.7 33.5 %all-to-all-start = ((bf16[32,2,64,128]{3,2,1,0:T(8,128)(2,1)}), bf16[32,2,64,128]{3,2,1,0:T(8,128)(2,1)S(1)}, u32[]{:S(2)}, u32[]{:S(2)}) async-start(bf16[32,2,64,128]{3,2,1,0:T(8,128)(2,1)} %bitcast.2), calls=%async_computation | async-start | bytes 2097152 | tf_op jit(solution)/shard_map/all_to_all | solution.py:570
  45.4 3.9 %collective-permute-start = (bf16[320,128]{1,0:T(8,128)(2,1)S(1)}, bf16[320,128]{1,0:T(8,128)(2,1)S(1)}, u32[]{:S(2)}, u32[]{:S(2)}) collective-permute-start(bf16[320,128]{1,0:T(8,128)(2,1)S(1)} %get-tuple-element.28), channel_id=1, source_target_pairs={{0,1},{1,2},{2,3},{3,0},{4,5},{5,6},{6,7},{7,4},{8,9},{9,10},{10,1... | collective-permute-start | bytes 245768 | tf_op jit(solution)/shard_map/ppermute | solution.py:45
  49.5 7.8 %collective-permute-start.1 = (bf16[2,64,512]{2,1,0:T(8,128)(2,1)S(1)}, bf16[2,64,512]{2,1,0:T(8,128)(2,1)S(1)}, u32[]{:S(2)}, u32[]{:S(2)}) collective-permute-start(bf16[2,64,512]{2,1,0:T(8,128)(2,1)S(1)} %get-tuple-element.34), channel_id=1, source_target_pairs={{0,4},{4,8},{8,12},{12,16},{16,20},{20,24},{24,28},{28,0},{1,5},{5... | collective-permute-start | bytes 393224 | tf_op jit(solution)/shard_map/ppermute | solution.py:45

commit v3 on v2

--- a/solution.py
+++ b/solution.py
@@ -244,6 +244,7 @@
         plan_ref[part + 1] = ((quad + STEP - 1) // STEP) * STEP
 
     full = ((quad + STEP - 1) // STEP) * STEP
+    plan_ref[2] = jnp.maximum(plan_ref[2], (full // STEP) * 3 // 7 * STEP)
 
     @pl.loop(quad, full)
     def _(i):

time: 59.1 us -> 59.6 us (level)
  Pallas kernels: 30 us -> 30.8 us
  transfers between devices with their start and end apart: 3 -> 3, of which waited for: 3 -> 3; matrix products, arithmetic and copies ran while one was open for 0% -> 0% of each run, Pallas kernels for 29% -> 30%
where the time goes in v3:
time: 59.6 us; the launch traced here: 58.9 us
  Pallas kernels  30.8 us (52%)
  waiting for transfers between devices  18.5 us (31%)
  starting transfers between devices  8.91 us (15%)
  between operations  0.73 us (1%)
    all_to_all x1, waiting for transfers between devices, shards(): lax.all_to_all(outgoing, both, split_axis=0, concat_axis=0, tiled=True)  13.2 us
    pallas_call x1, Pallas kernels, plan_blocks(): pl.pallas_call(functools.partial(plan_body, layout=layout, row_slots=row_...  12.4 us
    pallas_call x1, Pallas kernels, make_kernels(): pl.pallas_call(kernels_body, in_specs=[hbm] * 5, out_specs=pl.BlockSpec(m...  8.73 us
    pallas_call x3, Pallas kernels, grid_part(): pl.pallas_call(functools.partial(grid_body, part=part, first_part=first_p...  8.45 us
    all_to_all x1, starting transfers between devices, shards(): lax.all_to_all(outgoing, both, split_axis=0, concat_axis=0, tiled=True)  7.3 us
    ppermute x2, waiting for transfers between devices, around(): lax.ppermute(block, axis, [(i, (i + 1) % devices) for i in range(devices)])  5.24 us
    ppermute x2, starting transfers between devices, around(): lax.ppermute(block, axis, [(i, (i + 1) % devices) for i in range(devices)])  1.61 us
  transfers between devices with their start and end apart: 3, of which 3 were waited for; matrix products, arithmetic and copies ran while one was open for 0% of the time, Pallas kernels for 30%

profile of v3, /device:TPU:0, one launch (start us, length us, event | category | flops | bytes accessed | tf_op | source)
XLA Modules:
  0.0 58.9 jit_solution(7969878093920920434)
XLA Ops:
  0.0 0.0 copy-start
  0.0 0.0 copy-start.1
  0.0 8.7 %make_kernels.1 = bf16[64,64,128]{2,1,0:T(8,128)(2,1)} custom-call(s32[2,32]{1,0:T(2,128)} %bitcast.8, s32[1,32]{1,0:T(1,128)} %count_hbm.1, f32[4]{0:T(128)} %depth_hbm.1, bf16[4,512,512]{2,1,0:T(8,128)(2,1)} %amp_hbm.1, bf16[4,512,512]{2,1,0:T(8,128)(2,1)} %phase_hbm.1), custom_call_target="tpu_custom_call" | custom-call | tf_op jit(solution)/shard_map/make_kernels/pallas_call | solution.py:152
  8.7 7.3 %all-to-all-start = ((bf16[32,2,64,128]{3,2,1,0:T(8,128)(2,1)}), bf16[32,2,64,128]{3,2,1,0:T(8,128)(2,1)S(1)}, u32[]{:S(2)}, u32[]{:S(2)}) async-start(bf16[32,2,64,128]{3,2,1,0:T(8,128)(2,1)} %bitcast.2), calls=%async_computation | async-start | bytes 2097152 | tf_op jit(solution)/shard_map/all_to_all | solution.py:571
  16.7 0.0 copy-done
  16.7 0.0 copy-done.1
  16.7 12.4 %plan_blocks.1 = (s32[660]{0:T(1024)S(4)}, bf16[512,128,128]{2,1,0:T(8,128)(2,1)}, bf16[512,64,128]{2,1,0:T(8,128)(2,1)}) custom-call(s32[384]{0:T(512)S(1)} %copy-done, s32[384]{0:T(512)S(1)} %copy-done.1, s32[1]{0:T(128)S(6)} %copy.29.count_ref, bf16[384,128,128]{2,1,0:T(8,128)(2,1)} %left_hbm.1, bf16[384,64,128]{2,1,0:T(8,128)(2,1)} %right_hbm.1), custom_call_target="tpu_custom_call" | custom-call | tf_op jit(solution)/shard_map/plan_blocks/pallas_call | solution.py:300
  29.1 13.2 %all-to-all-done = bf16[32,2,64,128]{3,2,1,0:T(8,128)(2,1)S(1)} async-done(((bf16[32,2,64,128]{3,2,1,0:T(8,128)(2,1)}), bf16[32,2,64,128]{3,2,1,0:T(8,128)(2,1)S(1)}, u32[]{:S(2)}, u32[]{:S(2)}) %all-to-all-start) | async-done | bytes 1048608 | tf_op jit(solution)/shard_map/all_to_all | solution.py:571
  42.3 3.1 %grid_part.3 = (f32[32,128,256]{2,1,0:T(8,128)S(1)}, bf16[4,32,128,128]{3,2,1,0:T(8,128)(2,1)S(1)}, bf16[4,32,64,128]{3,2,1,0:T(8,128)(2,1)S(1)}, bf16[4,512,256]{2,1,0:T(8,128)(2,1)S(1)}, bf16[320,128]{1,0:T(8,128)(2,1)S(1)}) custom-call(s32[660]{0:T(1024)S(4)} %get-tuple-element.20.plan_ref, bf16[64,64,128]{2,1,0:T(8,128)(2,1)S(1)} %bitcast.5, ...), custom_call_target="tpu_custom_call" | custom-call | tf_op jit(solution)/shard_map/grid_part/pallas_call | solution.py:487
  45.4 0.1 collective-permute-start
  45.5 2.0 %grid_part.4 = (f32[32,128,256]{2,1,0:T(8,128)S(1)}, bf16[4,32,128,128]{3,2,1,0:T(8,128)(2,1)S(1)}, bf16[4,32,64,128]{3,2,1,0:T(8,128)(2,1)S(1)}, bf16[4,512,256]{2,1,0:T(8,128)(2,1)S(1)}) custom-call(s32[660]{0:T(1024)S(4)} %get-tuple-element.20.plan_ref, ...), custom_call_target="tpu_custom_call", output_to_operand_aliasing={{0}: (4, {}), {1}: (5, {}), {2}: (6, {}), {3}: (7, {})} | custom-call | tf_op jit(solution)/shard_map/grid_part/pallas_call | solution.py:487
  47.4 1.9 %collective-permute-done.col_ref = bf16[320,128]{1,0:T(8,128)(2,1)S(1)} collective-permute-done((bf16[320,128]{1,0:T(8,128)(2,1)S(1)}, bf16[320,128]{1,0:T(8,128)(2,1)S(1)}, u32[]{:S(2)}, u32[]{:S(2)}) %collective-permute-start) | collective-permute-done | bytes 81952 | tf_op jit(solution)/shard_map/ppermute | solution.py:45
  49.3 0.1 row_halo.1
  49.5 1.5 %collective-permute-start.1 = (bf16[2,64,512]{2,1,0:T(8,128)(2,1)S(1)}, bf16[2,64,512]{2,1,0:T(8,128)(2,1)S(1)}, u32[]{:S(2)}, u32[]{:S(2)}) collective-permute-start(bf16[2,64,512]{2,1,0:T(8,128)(2,1)S(1)} %get-tuple-element.34), channel_id=1, source_target_pairs={{0,4},{4,8},{8,12},{12,16},{16,20},{20,24},{24,28},{28,0},{1,5},{5... | collective-permute-start | bytes 393224 | tf_op jit(solution)/shard_map/ppermute | solution.py:45
  51.0 3.4 %grid_part.5 = (f32[32,128,256]{2,1,0:T(8,128)S(1)}, bf16[4,32,128,128]{3,2,1,0:T(8,128)(2,1)S(1)}, bf16[4,32,64,128]{3,2,1,0:T(8,128)(2,1)S(1)}, bf16[4,512,256]{2,1,0:T(8,128)(2,1)S(1)}) custom-call(s32[660]{0:T(1024)S(4)} %get-tuple-element.20.plan_ref, ...), custom_call_target="tpu_custom_call", output_to_operand_aliasing={{0}: (4, {}), {1}: (5, {}), {2}: (6, {}), {3}: (7, {})} | custom-call | tf_op jit(solution)/shard_map/grid_part/pallas_call | solution.py:487
  54.4 3.4 %collective-permute-done.1.row_ref = bf16[2,64,512]{2,1,0:T(8,128)(2,1)S(1)} collective-permute-done((bf16[2,64,512]{2,1,0:T(8,128)(2,1)S(1)}, bf16[2,64,512]{2,1,0:T(8,128)(2,1)S(1)}, u32[]{:S(2)}, u32[]{:S(2)}) %collective-permute-start.1) | collective-permute-done | bytes 131104 | tf_op jit(solution)/shard_map/ppermute | solution.py:45
  57.8 1.1 %merge_tile.1 = f32[2,256,512]{2,1,0:T(8,128)} custom-call(f32[32,128,256]{2,1,0:T(8,128)S(1)} %get-tuple-element.33.sums, bf16[2,64,512]{2,1,0:T(8,128)(2,1)S(1)} %collective-permute-done.1.row_ref, bf16[320,128]{1,0:T(8,128)(2,1)S(1)} %collective-permute-done.col_ref), custom_call_target="tpu_custom_call" | custom-call | tf_op jit(solution)/shard_map/merge_tile/pallas_call | solution.py:538
Async XLA Ops:
  0.0 16.7 %copy-start = (s32[384]{0:T(512)S(1)}, s32[384]{0:T(512)}, u32[]{:S(2)}) copy-start(s32[384]{0:T(512)} %pos_ref.1) | copy-start | bytes 4612
  0.0 16.7 %copy-start.1 = (s32[384]{0:T(512)S(1)}, s32[384]{0:T(512)}, u32[]{:S(2)}) copy-start(s32[384]{0:T(512)} %slot_ref.1) | copy-start | bytes 4612
  8.7 33.5 %all-to-all-start = ((bf16[32,2,64,128]{3,2,1,0:T(8,128)(2,1)}), bf16[32,2,64,128]{3,2,1,0:T(8,128)(2,1)S(1)}, u32[]{:S(2)}, u32[]{:S(2)}) async-start(bf16[32,2,64,128]{3,2,1,0:T(8,128)(2,1)} %bitcast.2), calls=%async_computation | async-start | bytes 2097152 | tf_op jit(solution)/shard_map/all_to_all | solution.py:571
  45.4 3.9 %collective-permute-start = (bf16[320,128]{1,0:T(8,128)(2,1)S(1)}, bf16[320,128]{1,0:T(8,128)(2,1)S(1)}, u32[]{:S(2)}, u32[]{:S(2)}) collective-permute-start(bf16[320,128]{1,0:T(8,128)(2,1)S(1)} %get-tuple-element.28), channel_id=1, source_target_pairs={{0,1},{1,2},{2,3},{3,0},{4,5},{5,6},{6,7},{7,4},{8,9},{9,10},{10,1... | collective-permute-start | bytes 245768 | tf_op jit(solution)/shard_map/ppermute | solution.py:45
  49.5 8.3 %collective-permute-start.1 = (bf16[2,64,512]{2,1,0:T(8,128)(2,1)S(1)}, bf16[2,64,512]{2,1,0:T(8,128)(2,1)S(1)}, u32[]{:S(2)}, u32[]{:S(2)}) collective-permute-start(bf16[2,64,512]{2,1,0:T(8,128)(2,1)S(1)} %get-tuple-element.34), channel_id=1, source_target_pairs={{0,4},{4,8},{8,12},{12,16},{16,20},{20,24},{24,28},{28,0},{1,5},{5... | collective-permute-start | bytes 393224 | tf_op jit(solution)/shard_map/ppermute | solution.py:45

commit v4 on v1

--- a/solution.py
+++ b/solution.py
@@ -40,10 +40,18 @@
     return horner(COS_POLY, u), x * horner(SIN_POLY, u)
 
 
-def from_behind(block, axis, distance):
-    devices = range(lax.axis_size(axis))
-    route = [(i - distance, i) for i in devices if i - distance in devices]
-    return lax.ppermute(block, axis, route)
+def around(block, axes):
+    sizes = [lax.axis_size(axis) for axis in axes]
+    route = []
+    for place in np.ndindex(*sizes):
+        target = [(i + 1) % n for i, n in zip(place, sizes)]
+        route.append((int(np.ravel_multi_index(place, sizes)), int(np.ravel_multi_index(target, sizes))))
+    return lax.ppermute(block, axes, route)
+
+
+def past_first(axes, halo):
+    real = functools.reduce(jnp.logical_and, [lax.axis_index(axis) > 0 for axis in axes])
+    return jnp.where(real, halo.astype(jnp.float32), 0.0)
 
 
 def in_hbm(array):
@@ -332,8 +340,10 @@
     if not first_part:
         rest = rest[4:]
     sums, left_ring, right_ring, ahead, *rest = rest
-    if first_part:
-        col_ref, *rest = rest
+    if part == 0:
+        col_ref, corner_ref, *rest = rest
+    if part == 1:
+        row_ref, *rest = rest
     behind_ref, sems = rest
     mixed = (ahead, behind_ref)
     slots, kernel_size, _ = kern_ref.shape
@@ -421,45 +431,26 @@
     wait(end, LEFT)
     wait(end + 1, LEFT)
     wait(end + 1, RIGHT)
-    if not first_part:
+    if part > 1:
         return
     low = lax.broadcasted_iota(jnp.int32, (kernel_size, patch), 1) < kernel_size
     take = functools.partial(strip, sums, row_slots, col_slots, kernel_size)
-    for a in range(row_slots + 1):
-        real = pltpu.roll(take(0, a, col_slots - 1), kernel_size, 1)
-        edge = jnp.where(low, real, take(1, a, col_slots - 1))
-        col_ref[a * kernel_size : (a + 1) * kernel_size, :] = edge.astype(col_ref.dtype)
-
-
-def row_body(before, col_ref, sums, row_ref, *, row_slots, col_slots):
-    kernel_size = row_ref.shape[1]
-    patch = sums.shape[1]
-    low = lax.broadcasted_iota(jnp.int32, (kernel_size, patch), 1) < kernel_size
-    take = functools.partial(strip, sums, row_slots, col_slots, kernel_size)
-    corner = col_ref[row_slots * kernel_size :, :].astype(jnp.float32)
+    if part == 0:
+        for a in range(row_slots + 1):
+            real = pltpu.roll(take(0, a, col_slots - 1), kernel_size, 1)
+            edge = jnp.where(low, real, take(1, a, col_slots - 1)).astype(col_ref.dtype)
+            if a < row_slots:
+                col_ref[a * kernel_size : (a + 1) * kernel_size, :] = edge
+            else:
+                corner_ref[...] = edge
+        return
     for plane in range(2):
-        behind = corner if plane == 0 else pltpu.roll(corner, kernel_size, 1)
+        behind = 0.0
         for tile in range(col_slots // 2):
             odd = pltpu.roll(take(plane, row_slots, 2 * tile + 1), kernel_size, 1)
             value = take(plane, row_slots, 2 * tile) + jnp.where(low, behind, odd)
             row_ref[plane, :, tile * patch : (tile + 1) * patch] = value.astype(row_ref.dtype)
             behind = odd
-
-
-def row_halo(sums, col, kernel_size):
-    vmem = pl.BlockSpec(memory_space=pltpu.VMEM)
-    return pl.pallas_call(
-        functools.partial(row_body, row_slots=TILE_U // kernel_size, col_slots=TILE_V // kernel_size),
-        in_specs=[vmem] * 2,
-        out_specs=[vmem] * 2,
-        out_shape=[
-            pltpu.VMEM(sums.shape, sums.dtype),
-            pltpu.VMEM((2, kernel_size, TILE_V), jnp.bfloat16),
-        ],
-        input_output_aliases={0: 0},
-        compiler_params=pltpu.CompilerParams(vmem_limit_bytes=4 * 2**20),
-        name="row_halo",
-    )(in_vmem(sums), in_vmem(col))
 
 
 def grid_part(plan, part, kernels, left, right, carried, layout):
@@ -478,8 +469,11 @@
         pltpu.VMEM((RING, STEP * QUAD) + right.shape[1:], right.dtype),
         pltpu.VMEM(mixed_shape, jnp.bfloat16),
     ]
-    if first_part:
-        out_shape.append(pltpu.VMEM((TILE_U + kernel_size, 2 * kernel_size), jnp.bfloat16))
+    if part == 0:
+        out_shape.append(pltpu.VMEM((TILE_U, 2 * kernel_size), jnp.bfloat16))
+        out_shape.append(pltpu.VMEM((kernel_size, 2 * kernel_size), jnp.bfloat16))
+    if part == 1:
+        out_shape.append(pltpu.VMEM((2, kernel_size, TILE_V), jnp.bfloat16))
     out = pl.pallas_call(
         functools.partial(
             grid_body,
@@ -498,12 +492,13 @@
             pltpu.SemaphoreType.DMA((2, RING)),
         ],
         compiler_params=pltpu.CompilerParams(vmem_limit_bytes=12 * 2**20),
+        cost_estimate=pl.CostEstimate(flops=2 * 10**9, bytes_accessed=10**7, transcendentals=0),
         name="grid_part",
     )(in_smem(plan), in_vmem(kernels), in_hbm(left), in_hbm(right), *carried)
     return out[:4], out[4:]
 
 
-def merge_body(sums, row_ref, col_ref, out_hbm, out_ref, sems):
+def merge_body(sums, row_ref, col_ref, corner_ref, out_hbm, out_ref, sems):
     kernel_size = row_ref.shape[1]
     patch = sums.shape[1]
     row_slots = out_ref.shape[1] // kernel_size
@@ -512,7 +507,9 @@
     take = functools.partial(strip, sums, row_slots, col_slots, kernel_size)
     for a in range(row_slots):
         rows = slice(a * kernel_size, (a + 1) * kernel_size)
-        edge = col_ref[rows, :].astype(jnp.float32)
+        edge = past_first(["tv"], col_ref[rows, :])
+        if a == 0:
+            edge = edge + past_first(["tu", "tv"], corner_ref[...])
         for plane in range(2):
             behind = edge if plane == 0 else pltpu.roll(edge, kernel_size, 1)
             for tile in range(col_slots // 2):
@@ -520,7 +517,7 @@
                 odd = pltpu.roll(take(plane, a, 2 * tile + 1), kernel_size, 1)
                 value = take(plane, a, 2 * tile) + jnp.where(low, behind, odd)
                 if a == 0:
-                    value = value + row_ref[plane, :, lanes].astype(jnp.float32)
+                    value = value + past_first(["tu"], row_ref[plane, :, lanes])
                 out_ref[plane, rows, lanes] = value
                 behind = odd
         pltpu.make_async_copy(out_ref.at[:, rows], out_hbm.at[:, rows], sems.at[a]).start()
@@ -529,11 +526,11 @@
         pltpu.make_async_copy(out_ref.at[:, rows], out_hbm.at[:, rows], sems.at[a]).wait()
 
 
-def merge_tile(sums, row, col):
+def merge_tile(sums, row, col, corner):
     vmem = pl.BlockSpec(memory_space=pltpu.VMEM)
     return pl.pallas_call(
         merge_body,
-        in_specs=[vmem] * 3,
+        in_specs=[vmem] * 4,
         out_specs=pl.BlockSpec(memory_space=pl.ANY),
         out_shape=jax.ShapeDtypeStruct((2, TILE_U, TILE_V), jnp.float32),
         scratch_shapes=[
@@ -542,7 +539,7 @@
         ],
         compiler_params=pltpu.CompilerParams(vmem_limit_bytes=8 * 2**20),
         name="merge_tile",
-    )(*map(in_vmem, (sums, row, col)))
+    )(*map(in_vmem, (sums, row, col, corner)))
 
 
 def shards(
@@ -568,13 +565,13 @@
     received = arrived.reshape((-1,) + arrived.shape[2:])
     layout = Layout(block_pos.shape[0], (TILE_U // kernel_size) * (TILE_V // kernel_size))
     plan, left, right = plan_blocks(block_pos, block_slot, block_count, vis_left, vis_right, layout)
-    carried, (col,) = grid_part(plan, 0, received, left, right, None, layout)
-    col = from_behind(col, "tv", 1)
-    carried, _ = grid_part(plan, 1, received, left, right, carried, layout)
-    sums, row = row_halo(carried[0], col, kernel_size)
-    row = from_behind(row, "tu", 1)
-    carried, _ = grid_part(plan, 2, received, left, right, [sums, *carried[1:]], layout)
-    return merge_tile(carried[0], row, col)
+    carried, (col, corner) = grid_part(plan, 0, received, left, right, None, layout)
+    col = around(col, ("tv",))
+    corner = around(corner, ("tu", "tv"))
+    carried, (row,) = grid_part(plan, 1, received, left, right, carried, layout)
+    row = around(row, ("tu",))
+    carried, _ = grid_part(plan, 2, received, left, right, carried, layout)
+    return merge_tile(carried[0], row, col, corner)
 
 
 def solution(mesh):

time: 62.7 us -> 60.2 us (0.960)
  the two profiles are of different devices: /device:TPU:1 before, /device:TPU:0 now
where the time goes in v4:
time: 60.2 us; the launch traced here: 59.4 us
  Pallas kernels  32.1 us (53%)
  waiting for transfers between devices  16.2 us (27%)
  starting transfers between devices  10.4 us (17%)
  between operations  0.74 us (1%)
    pallas_call x1, Pallas kernels, plan_blocks(): pl.pallas_call(functools.partial(plan_body, layout=layout, row_slots=row_...  13.6 us
    all_to_all x1, waiting for transfers between devices, shards(): lax.all_to_all(outgoing, both, split_axis=0, concat_axis=0, tiled=True)  12 us
    pallas_call x1, Pallas kernels, make_kernels(): pl.pallas_call(kernels_body, in_specs=[hbm] * 5, out_specs=pl.BlockSpec(m...  8.73 us
    pallas_call x3, Pallas kernels, grid_part(): pl.pallas_call(functools.partial(grid_body, part=part, first_part=first_p...  8.61 us
    all_to_all x1, starting transfers between devices, shards(): lax.all_to_all(outgoing, both, split_axis=0, concat_axis=0, tiled=True)  7.3 us
    ppermute x3, waiting for transfers between devices, around(): return lax.ppermute(block, axes, route)  4.24 us
    ppermute x3, starting transfers between devices, around(): return lax.ppermute(block, axes, route)  3.08 us
  transfers between devices with their start and end apart: 4, of which 2 were waited for; matrix products, arithmetic and copies ran while one was open for 0% of the time, Pallas kernels for 32%

profile of v4, /device:TPU:0, one launch (start us, length us, event | category | flops | bytes accessed | tf_op | source)
XLA Modules:
  0.0 59.4 jit_solution(1193437204979738444)
XLA Ops:
  0.0 0.0 copy-start
  0.0 0.0 copy-start.1
  0.0 8.7 %make_kernels.1 = bf16[64,64,128]{2,1,0:T(8,128)(2,1)} custom-call(s32[2,32]{1,0:T(2,128)} %bitcast.8, s32[1,32]{1,0:T(1,128)} %count_hbm.1, f32[4]{0:T(128)} %depth_hbm.1, bf16[4,512,512]{2,1,0:T(8,128)(2,1)} %amp_hbm.1, bf16[4,512,512]{2,1,0:T(8,128)(2,1)} %phase_hbm.1), custom_call_target="tpu_custom_call" | custom-call | tf_op jit(solution)/shard_map/make_kernels/pallas_call | solution.py:157
  8.7 7.3 %all-to-all-start = ((bf16[32,2,64,128]{3,2,1,0:T(8,128)(2,1)}), bf16[32,2,64,128]{3,2,1,0:T(8,128)(2,1)S(1)}, u32[]{:S(2)}, u32[]{:S(2)}) async-start(bf16[32,2,64,128]{3,2,1,0:T(8,128)(2,1)} %bitcast.2), calls=%async_computation | async-start | bytes 2097152 | tf_op jit(solution)/shard_map/all_to_all | solution.py:564
  16.7 0.0 copy-done
  16.7 0.0 copy-done.1
  16.7 13.6 %plan_blocks.1 = (s32[660]{0:T(1024)S(4)}, bf16[512,128,128]{2,1,0:T(8,128)(2,1)}, bf16[512,64,128]{2,1,0:T(8,128)(2,1)}) custom-call(s32[384]{0:T(512)S(1)} %copy-done, s32[384]{0:T(512)S(1)} %copy-done.1, s32[1]{0:T(128)S(6)} %copy.27.count_ref, bf16[384,128,128]{2,1,0:T(8,128)(2,1)} %left_hbm.1, bf16[384,64,128]{2,1,0:T(8,128)(2,1)} %right_hbm.1), custom_call_target="tpu_custom_call" | custom-call | tf_op jit(solution)/shard_map/plan_blocks/pallas_call | solution.py:304
  30.3 12.0 %all-to-all-done = bf16[32,2,64,128]{3,2,1,0:T(8,128)(2,1)S(1)} async-done(((bf16[32,2,64,128]{3,2,1,0:T(8,128)(2,1)}), bf16[32,2,64,128]{3,2,1,0:T(8,128)(2,1)S(1)}, u32[]{:S(2)}, u32[]{:S(2)}) %all-to-all-start) | async-done | bytes 1048608 | tf_op jit(solution)/shard_map/all_to_all | solution.py:564
  42.3 3.2 %grid_part.3 = (f32[32,128,256]{2,1,0:T(8,128)S(1)}, bf16[4,32,128,128]{3,2,1,0:T(8,128)(2,1)S(1)}, bf16[4,32,64,128]{3,2,1,0:T(8,128)(2,1)S(1)}, bf16[4,512,256...) custom-call(s32[660]{0:T(1024)S(4)} %get-tuple-element.20.plan_ref, ...), custom_call_target="tpu_custom_call" | custom-call | flops 2000000000 | bytes 10000000 | tf_op jit(solution)/shard_map/grid_part/pallas_call | solution.py:477
  45.4 1.0 %collective-permute-start.2 = (bf16[64,128]{1,0:T(8,128)(2,1)S(1)}, bf16[64,128]{1,0:T(8,128)(2,1)S(1)}, u32[]{:S(2)}, u32[]{:S(2)}) collective-permute-start(bf16[64,128]{1,0:T(8,128)(2,1)S(1)} %get-tuple-element.34), channel_id=1, source_target_pairs={{0,5},{1,6},{2,7},{3,4},{4,9},{5,10},{6,11},{7,8},{8,13},{9,14},{1... | collective-permute-start | bytes 49160 | tf_op jit(solution)/shard_map/ppermute | solution.py:49
  46.5 2.0 %collective-permute-start.1 = (bf16[256,128]{1,0:T(8,128)(2,1)S(1)}, bf16[256,128]{1,0:T(8,128)(2,1)S(1)}, u32[]{:S(2)}, u32[]{:S(2)}) collective-permute-start(bf16[256,128]{1,0:T(8,128)(2,1)S(1)} %get-tuple-element.33), channel_id=1, source_target_pairs={{0,1},{1,2},{2,3},{3,0},{4,5},{5,6},{6,7},{7,4},{8,9},{9,10},{10,1... | collective-permute-start | bytes 196616 | tf_op jit(solution)/shard_map/ppermute | solution.py:49
  48.5 2.1 %grid_part.4 = (f32[32,128,256]{2,1,0:T(8,128)S(1)}, bf16[4,32,128,128]{3,2,1,0:T(8,128)(2,1)S(1)}, bf16[4,32,64,128]{3,2,1,0:T(8,128)(2,1)S(1)}, bf16[4,512,256...) custom-call(s32[660]{0:T(1024)S(4)} %get-tuple-element.20.plan_ref, ...), custom_call_target="tpu_custom_call", output_to_operand_aliasing={{0}: (4, {}), {1}: (5, {}), {2}: (6, {}), {3}: (7, {})} | custom-call | flops 2000000000 | bytes 10000000 | tf_op jit(solution)/shard_map/grid_part/pallas_call | solution.py:477
  50.5 0.1 collective-permute-start
  50.6 3.4 %grid_part.5 = (f32[32,128,256]{2,1,0:T(8,128)S(1)}, bf16[4,32,128,128]{3,2,1,0:T(8,128)(2,1)S(1)}, bf16[4,32,64,128]{3,2,1,0:T(8,128)(2,1)S(1)}, bf16[4,512,256]{2,1,0:T(8,128)(2,1)S(1)}) custom-call(s32[660]{0:T(1024)S(4)} %get-tuple-element.20.plan_ref, ...), custom_call_target="tpu_custom_call", output_to_operand_aliasing={{0}: (4, {}), {1}: (5, {}), {2}: (6, {}), {3}: (7, {})} | custom-call | flops 2000000000 | bytes 10000000 | tf_op jit(solution)/shard_map/grid_part/pallas_call | solution.py:477
  54.0 0.0 collective-permute-done.2.corner_ref
  54.0 0.0 collective-permute-done.1.col_ref
  54.0 4.2 %collective-permute-done.row_ref = bf16[2,64,512]{2,1,0:T(8,128)(2,1)S(1)} collective-permute-done((bf16[2,64,512]{2,1,0:T(8,128)(2,1)S(1)}, bf16[2,64,512]{2,1,0:T(8,128)(2,1)S(1)}, u32[]{:S(2)}, u32[]{:S(2)}) %collective-permute-start) | collective-permute-done | bytes 131104 | tf_op jit(solution)/shard_map/ppermute | solution.py:49
  58.3 1.1 %merge_tile.1 = f32[2,256,512]{2,1,0:T(8,128)} custom-call(f32[32,128,256]{2,1,0:T(8,128)S(1)} %get-tuple-element.31.sums, bf16[2,64,512]{2,1,0:T(8,128)(2,1)S(1)} %collective-permute-done.row_ref, bf16[256,128]{1,0:T(8,128)(2,1)S(1)} %collective-permute-done.1.col_ref, bf16[64,128]{1,0:T(8,128)(2,1)S(1)} %collective-permute-done.2.corner_ref), custom_call_target="tpu_custom_call" | custom-call | tf_op jit(solution)/shard_map/merge_tile/pallas_call | solution.py:531
Async XLA Ops:
  0.0 16.7 %copy-start = (s32[384]{0:T(512)S(1)}, s32[384]{0:T(512)}, u32[]{:S(2)}) copy-start(s32[384]{0:T(512)} %pos_ref.1) | copy-start | bytes 4612
  0.0 16.7 %copy-start.1 = (s32[384]{0:T(512)S(1)}, s32[384]{0:T(512)}, u32[]{:S(2)}) copy-start(s32[384]{0:T(512)} %slot_ref.1) | copy-start | bytes 4612
  8.7 33.5 %all-to-all-start = ((bf16[32,2,64,128]{3,2,1,0:T(8,128)(2,1)}), bf16[32,2,64,128]{3,2,1,0:T(8,128)(2,1)S(1)}, u32[]{:S(2)}, u32[]{:S(2)}) async-start(bf16[32,2,64,128]{3,2,1,0:T(8,128)(2,1)} %bitcast.2), calls=%async_computation | async-start | bytes 2097152 | tf_op jit(solution)/shard_map/all_to_all | solution.py:564
  45.4 8.6 %collective-permute-start.2 = (bf16[64,128]{1,0:T(8,128)(2,1)S(1)}, bf16[64,128]{1,0:T(8,128)(2,1)S(1)}, u32[]{:S(2)}, u32[]{:S(2)}) collective-permute-start(bf16[64,128]{1,0:T(8,128)(2,1)S(1)} %get-tuple-element.34), channel_id=1, source_target_pairs={{0,5},{1,6},{2,7},{3,4},{4,9},{5,10},{6,11},{7,8},{8,13},{9,14},{1... | collective-permute-start | bytes 49160 | tf_op jit(solution)/shard_map/ppermute | solution.py:49
  46.5 7.5 %collective-permute-start.1 = (bf16[256,128]{1,0:T(8,128)(2,1)S(1)}, bf16[256,128]{1,0:T(8,128)(2,1)S(1)}, u32[]{:S(2)}, u32[]{:S(2)}) collective-permute-start(bf16[256,128]{1,0:T(8,128)(2,1)S(1)} %get-tuple-element.33), channel_id=1, source_target_pairs={{0,1},{1,2},{2,3},{3,0},{4,5},{5,6},{6,7},{7,4},{8,9},{9,10},{10,1... | collective-permute-start | bytes 196616 | tf_op jit(solution)/shard_map/ppermute | solution.py:49
  50.5 7.7 %collective-permute-start = (bf16[2,64,512]{2,1,0:T(8,128)(2,1)S(1)}, bf16[2,64,512]{2,1,0:T(8,128)(2,1)S(1)}, u32[]{:S(2)}, u32[]{:S(2)}) collective-permute-start(bf16[2,64,512]{2,1,0:T(8,128)(2,1)S(1)} %get-tuple-element.32), channel_id=1, source_target_pairs={{0,4},{4,8},{8,12},{12,16},{16,20},{20,24},{24,28},{28,0},{1,5},{5... | collective-permute-start | bytes 393224 | tf_op jit(solution)/shard_map/ppermute | solution.py:49

commit v5 on v4

--- a/solution.py
+++ b/solution.py
@@ -179,7 +179,7 @@
 
 class Layout:
     def __init__(self, blocks, anchors):
-        self.parts = 3
+        self.parts = 2
         quads = (blocks + (QUAD - 1) * anchors) // QUAD + 1
         self.quads = (quads + STEP - 1) // STEP * STEP
         self.anchor = self.parts + 1
@@ -243,7 +243,7 @@
     quad = 0
     begin = 0
     plan_ref[0] = 0
-    for part, end in enumerate([row_slots, border, anchors]):
+    for part, end in enumerate([border, anchors]):
         quad = lax.fori_loop(begin, end, lay, quad)
         begin = end
         plan_ref[part + 1] = ((quad + STEP - 1) // STEP) * STEP
@@ -340,10 +340,8 @@
     if not first_part:
         rest = rest[4:]
     sums, left_ring, right_ring, ahead, *rest = rest
-    if part == 0:
-        col_ref, corner_ref, *rest = rest
-    if part == 1:
-        row_ref, *rest = rest
+    if first_part:
+        row_ref, col_ref, corner_ref, *rest = rest
     behind_ref, sems = rest
     mixed = (ahead, behind_ref)
     slots, kernel_size, _ = kern_ref.shape
@@ -431,19 +429,17 @@
     wait(end, LEFT)
     wait(end + 1, LEFT)
     wait(end + 1, RIGHT)
-    if part > 1:
+    if not first_part:
         return
     low = lax.broadcasted_iota(jnp.int32, (kernel_size, patch), 1) < kernel_size
     take = functools.partial(strip, sums, row_slots, col_slots, kernel_size)
-    if part == 0:
-        for a in range(row_slots + 1):
-            real = pltpu.roll(take(0, a, col_slots - 1), kernel_size, 1)
-            edge = jnp.where(low, real, take(1, a, col_slots - 1)).astype(col_ref.dtype)
-            if a < row_slots:
-                col_ref[a * kernel_size : (a + 1) * kernel_size, :] = edge
-            else:
-                corner_ref[...] = edge
-        return
+    for a in range(row_slots + 1):
+        real = pltpu.roll(take(0, a, col_slots - 1), kernel_size, 1)
+        edge = jnp.where(low, real, take(1, a, col_slots - 1)).astype(col_ref.dtype)
+        if a < row_slots:
+            col_ref[a * kernel_size : (a + 1) * kernel_size, :] = edge
+        else:
+            corner_ref[...] = edge
     for plane in range(2):
         behind = 0.0
         for tile in range(col_slots // 2):
@@ -469,11 +465,12 @@
         pltpu.VMEM((RING, STEP * QUAD) + right.shape[1:], right.dtype),
         pltpu.VMEM(mixed_shape, jnp.bfloat16),
     ]
-    if part == 0:
-        out_shape.append(pltpu.VMEM((TILE_U, 2 * kernel_size), jnp.bfloat16))
-        out_shape.append(pltpu.VMEM((kernel_size, 2 * kernel_size), jnp.bfloat16))
-    if part == 1:
-        out_shape.append(pltpu.VMEM((2, kernel_size, TILE_V), jnp.bfloat16))
+    if first_part:
+        out_shape += [
+            pltpu.VMEM((2, kernel_size, TILE_V), jnp.bfloat16),
+            pltpu.VMEM((TILE_U, 2 * kernel_size), jnp.bfloat16),
+            pltpu.VMEM((kernel_size, 2 * kernel_size), jnp.bfloat16),
+        ]
     out = pl.pallas_call(
         functools.partial(
             grid_body,
@@ -565,12 +562,11 @@
     received = arrived.reshape((-1,) + arrived.shape[2:])
     layout = Layout(block_pos.shape[0], (TILE_U // kernel_size) * (TILE_V // kernel_size))
     plan, left, right = plan_blocks(block_pos, block_slot, block_count, vis_left, vis_right, layout)
-    carried, (col, corner) = grid_part(plan, 0, received, left, right, None, layout)
+    carried, (row, col, corner) = grid_part(plan, 0, received, left, right, None, layout)
+    row = around(row, ("tu",))
     col = around(col, ("tv",))
     corner = around(corner, ("tu", "tv"))
-    carried, (row,) = grid_part(plan, 1, received, left, right, carried, layout)
-    row = around(row, ("tu",))
-    carried, _ = grid_part(plan, 2, received, left, right, carried, layout)
+    carried, _ = grid_part(plan, 1, received, left, right, carried, layout)
     return merge_tile(carried[0], row, col, corner)
 
 

time: 60.2 us -> 60.3 us (level)
  Pallas kernels: 32.1 us -> 29.1 us
  starting transfers between devices: 10.4 us -> 12.3 us
  waiting for transfers between devices: 16.2 us -> 17.8 us
    ppermute x3, starting transfers between devices: 3.08 us -> 5.03 us  [around(): return lax.ppermute(block, axes, route)]
    pallas_call x3 -> x2, Pallas kernels: 8.61 us -> 7.04 us  [grid_part(): pl.pallas_call(functools.partial(grid_body, part=part, first_part=first_p...]
    all_to_all x1, waiting for transfers between devices: 12 us -> 13.3 us  [shards(): lax.all_to_all(outgoing, both, split_axis=0, concat_axis=0, tiled=True)]
    pallas_call x1, Pallas kernels: 13.6 us -> 12.2 us  [plan_blocks(): pl.pallas_call(functools.partial(plan_body, layout=layout, row_slots=row_...]
  transfers between devices with their start and end apart: 4 -> 4, of which waited for: 2 -> 2; matrix products, arithmetic and copies ran while one was open for 0% -> 0% of each run, Pallas kernels for 32% -> 26%
where the time goes in v5:
time: 60.3 us; the launch traced here: 60 us
  Pallas kernels  29.1 us (48%)
  waiting for transfers between devices  17.8 us (30%)
  starting transfers between devices  12.3 us (20%)
  between operations  0.72 us (1%)
    all_to_all x1, waiting for transfers between devices, shards(): lax.all_to_all(outgoing, both, split_axis=0, concat_axis=0, tiled=True)  13.3 us
    pallas_call x1, Pallas kernels, plan_blocks(): pl.pallas_call(functools.partial(plan_body, layout=layout, row_slots=row_...  12.2 us
    pallas_call x1, Pallas kernels, make_kernels(): pl.pallas_call(kernels_body, in_specs=[hbm] * 5, out_specs=pl.BlockSpec(m...  8.73 us
    all_to_all x1, starting transfers between devices, shards(): lax.all_to_all(outgoing, both, split_axis=0, concat_axis=0, tiled=True)  7.3 us
    pallas_call x2, Pallas kernels, grid_part(): pl.pallas_call(functools.partial(grid_body, part=part, first_part=first_p...  7.04 us
    ppermute x3, starting transfers between devices, around(): return lax.ppermute(block, axes, route)  5.03 us
    ppermute x3, waiting for transfers between devices, around(): return lax.ppermute(block, axes, route)  4.45 us
  transfers between devices with their start and end apart: 4, of which 2 were waited for; matrix products, arithmetic and copies ran while one was open for 0% of the time, Pallas kernels for 26%

profile of v5, /device:TPU:0, one launch (start us, length us, event | category | flops | bytes accessed | tf_op | source)
XLA Modules:
  0.0 60.0 jit_solution(10156785914376646321)
XLA Ops:
  0.0 0.0 copy-start
  0.0 0.0 copy-start.1
  0.0 8.7 %make_kernels.1 = bf16[64,64,128]{2,1,0:T(8,128)(2,1)} custom-call(s32[2,32]{1,0:T(2,128)} %bitcast.7, s32[1,32]{1,0:T(1,128)} %count_hbm.1, f32[4]{0:T(128)} %depth_hbm.1, bf16[4,512,512]{2,1,0:T(8,128)(2,1)} %amp_hbm.1, bf16[4,512,512]{2,1,0:T(8,128)(2,1)} %phase_hbm.1), custom_call_target="tpu_custom_call" | custom-call | tf_op jit(solution)/shard_map/make_kernels/pallas_call | solution.py:157
  8.7 7.3 %all-to-all-start = ((bf16[32,2,64,128]{3,2,1,0:T(8,128)(2,1)}), bf16[32,2,64,128]{3,2,1,0:T(8,128)(2,1)S(1)}, u32[]{:S(2)}, u32[]{:S(2)}) async-start(bf16[32,2,64,128]{3,2,1,0:T(8,128)(2,1)} %bitcast.2), calls=%async_computation | async-start | bytes 2097152 | tf_op jit(solution)/shard_map/all_to_all | solution.py:561
  16.7 0.0 copy-done
  16.7 0.0 copy-done.1
  16.7 12.2 %plan_blocks.1 = (s32[659]{0:T(1024)S(4)}, bf16[512,128,128]{2,1,0:T(8,128)(2,1)}, bf16[512,64,128]{2,1,0:T(8,128)(2,1)}) custom-call(s32[384]{0:T(512)S(1)} %copy-done, s32[384]{0:T(512)S(1)} %copy-done.1, s32[1]{0:T(128)S(6)} %copy.19.count_ref, bf16[384,128,128]{2,1,0:T(8,128)(2,1)} %left_hbm.1, bf16[384,64,128]{2,1,0:T(8,128)(2,1)} %right_hbm.1), custom_call_target="tpu_custom_call" | custom-call | tf_op jit(solution)/shard_map/plan_blocks/pallas_call | solution.py:304
  28.9 13.3 %all-to-all-done = bf16[32,2,64,128]{3,2,1,0:T(8,128)(2,1)S(1)} async-done(((bf16[32,2,64,128]{3,2,1,0:T(8,128)(2,1)}), bf16[32,2,64,128]{3,2,1,0:T(8,128)(2,1)S(1)}, u32[]{:S(2)}, u32[]{:S(2)}) %all-to-all-start) | async-done | bytes 1048608 | tf_op jit(solution)/shard_map/all_to_all | solution.py:561
  42.3 3.7 %grid_part.2 = (f32[32,128,256]{2,1,0:T(8,128)S(1)}, bf16[4,32,128,128]{3,2,1,0:T(8,128)(2,1)S(1)}, bf16[4,32,64,128]{3,2,1,0:T(8,128)(2,1)S(1)}, bf16[4,512,256...) custom-call(s32[659]{0:T(1024)S(4)} %get-tuple-element.16.plan_ref, ...), custom_call_target="tpu_custom_call" | custom-call | flops 2000000000 | bytes 10000000 | tf_op jit(solution)/shard_map/grid_part/pallas_call | solution.py:474
  46.0 0.6 collective-permute-start.2
  46.6 4.2 %collective-permute-start.1 = (bf16[256,128]{1,0:T(8,128)(2,1)S(1)}, bf16[256,128]{1,0:T(8,128)(2,1)S(1)}, u32[]{:S(2)}, u32[]{:S(2)}) collective-permute-start(bf16[256,128]{1,0:T(8,128)(2,1)S(1)} %get-tuple-element.25), channel_id=1, source_target_pairs={{0,1},{1,2},{2,3},{3,0},{4,5},{5,6},{6,7},{7,4},{8,9},{9,10},{10,1... | collective-permute-start | bytes 196616 | tf_op jit(solution)/shard_map/ppermute | solution.py:49
  50.7 0.3 collective-permute-start
  51.0 3.4 %grid_part.3 = (f32[32,128,256]{2,1,0:T(8,128)S(1)}, bf16[4,32,128,128]{3,2,1,0:T(8,128)(2,1)S(1)}, bf16[4,32,64,128]{3,2,1,0:T(8,128)(2,1)S(1)}, bf16[4,512,256]{2,1,0:T(8,128)(2,1)S(1)}) custom-call(s32[659]{0:T(1024)S(4)} %get-tuple-element.16.plan_ref, ...), custom_call_target="tpu_custom_call", output_to_operand_aliasing={{0}: (4, {}), {1}: (5, {}), {2}: (6, {}), {3}: (7, {})} | custom-call | flops 2000000000 | bytes 10000000 | tf_op jit(solution)/shard_map/grid_part/pallas_call | solution.py:474
  54.4 0.0 collective-permute-done.2.corner_ref
  54.4 0.0 collective-permute-done.1.col_ref
  54.4 4.4 %collective-permute-done.row_ref = bf16[2,64,512]{2,1,0:T(8,128)(2,1)S(1)} collective-permute-done((bf16[2,64,512]{2,1,0:T(8,128)(2,1)S(1)}, bf16[2,64,512]{2,1,0:T(8,128)(2,1)S(1)}, u32[]{:S(2)}, u32[]{:S(2)}) %collective-permute-start) | collective-permute-done | bytes 131104 | tf_op jit(solution)/shard_map/ppermute | solution.py:49
  58.8 1.1 %merge_tile.1 = f32[2,256,512]{2,1,0:T(8,128)} custom-call(f32[32,128,256]{2,1,0:T(8,128)S(1)} %get-tuple-element.23.sums, bf16[2,64,512]{2,1,0:T(8,128)(2,1)S(1)} %collective-permute-done.row_ref, bf16[256,128]{1,0:T(8,128)(2,1)S(1)} %collective-permute-done.1.col_ref, bf16[64,128]{1,0:T(8,128)(2,1)S(1)} %collective-permute-done.2.corner_ref), custom_call_target="tpu_custom_call" | custom-call | tf_op jit(solution)/shard_map/merge_tile/pallas_call | solution.py:528
Async XLA Ops:
  0.0 16.7 %copy-start = (s32[384]{0:T(512)S(1)}, s32[384]{0:T(512)}, u32[]{:S(2)}) copy-start(s32[384]{0:T(512)} %pos_ref.1) | copy-start | bytes 4612
  0.0 16.7 %copy-start.1 = (s32[384]{0:T(512)S(1)}, s32[384]{0:T(512)}, u32[]{:S(2)}) copy-start(s32[384]{0:T(512)} %slot_ref.1) | copy-start | bytes 4612
  8.7 33.5 %all-to-all-start = ((bf16[32,2,64,128]{3,2,1,0:T(8,128)(2,1)}), bf16[32,2,64,128]{3,2,1,0:T(8,128)(2,1)S(1)}, u32[]{:S(2)}, u32[]{:S(2)}) async-start(bf16[32,2,64,128]{3,2,1,0:T(8,128)(2,1)} %bitcast.2), calls=%async_computation | async-start | bytes 2097152 | tf_op jit(solution)/shard_map/all_to_all | solution.py:561
  46.0 8.4 %collective-permute-start.2 = (bf16[64,128]{1,0:T(8,128)(2,1)S(1)}, bf16[64,128]{1,0:T(8,128)(2,1)S(1)}, u32[]{:S(2)}, u32[]{:S(2)}) collective-permute-start(bf16[64,128]{1,0:T(8,128)(2,1)S(1)} %get-tuple-element.26), channel_id=1, source_target_pairs={{0,5},{1,6},{2,7},{3,4},{4,9},{5,10},{6,11},{7,8},{8,13},{9,14},{1... | collective-permute-start | bytes 49160 | tf_op jit(solution)/shard_map/ppermute | solution.py:49
  46.6 7.8 %collective-permute-start.1 = (bf16[256,128]{1,0:T(8,128)(2,1)S(1)}, bf16[256,128]{1,0:T(8,128)(2,1)S(1)}, u32[]{:S(2)}, u32[]{:S(2)}) collective-permute-start(bf16[256,128]{1,0:T(8,128)(2,1)S(1)} %get-tuple-element.25), channel_id=1, source_target_pairs={{0,1},{1,2},{2,3},{3,0},{4,5},{5,6},{6,7},{7,4},{8,9},{9,10},{10,1... | collective-permute-start | bytes 196616 | tf_op jit(solution)/shard_map/ppermute | solution.py:49
  50.7 8.1 %collective-permute-start = (bf16[2,64,512]{2,1,0:T(8,128)(2,1)S(1)}, bf16[2,64,512]{2,1,0:T(8,128)(2,1)S(1)}, u32[]{:S(2)}, u32[]{:S(2)}) collective-permute-start(bf16[2,64,512]{2,1,0:T(8,128)(2,1)S(1)} %get-tuple-element.24), channel_id=1, source_target_pairs={{0,4},{4,8},{8,12},{12,16},{16,20},{20,24},{24,28},{28,0},{1,5},{5... | collective-permute-start | bytes 393224 | tf_op jit(solution)/shard_map/ppermute | solution.py:49

commit v6 on v5

--- a/solution.py
+++ b/solution.py
@@ -489,7 +489,6 @@
             pltpu.SemaphoreType.DMA((2, RING)),
         ],
         compiler_params=pltpu.CompilerParams(vmem_limit_bytes=12 * 2**20),
-        cost_estimate=pl.CostEstimate(flops=2 * 10**9, bytes_accessed=10**7, transcendentals=0),
         name="grid_part",
     )(in_smem(plan), in_vmem(kernels), in_hbm(left), in_hbm(right), *carried)
     return out[:4], out[4:]

time: 60.3 us -> 58.2 us (0.965); the launches traced: 60 us -> 57.2 us
  waiting for transfers between devices: 17.8 us -> 11.2 us
  Pallas kernels: 29.1 us -> 32.8 us
    ppermute x3, waiting for transfers between devices: 4.45 us -> 0.01 us  [around(): return lax.ppermute(block, axes, route)]
    pallas_call x1, Pallas kernels: 12.2 us -> 14.4 us  [plan_blocks(): pl.pallas_call(functools.partial(plan_body, layout=layout, row_slots=row_...]
    all_to_all x1, waiting for transfers between devices: 13.3 us -> 11.1 us  [shards(): lax.all_to_all(outgoing, both, split_axis=0, concat_axis=0, tiled=True)]
    pallas_call x2, Pallas kernels: 7.04 us -> 8.49 us  [grid_part(): pl.pallas_call(functools.partial(grid_body, part=part, first_part=first_p...]
  transfers between devices with their start and end apart: 4 -> 4, of which waited for: 2 -> 1; matrix products, arithmetic and copies ran while one was open for 0% -> 0% of each run, Pallas kernels for 26% -> 32%
where the time goes in v6:
time: 58.2 us; the launch traced here: 57.2 us
  Pallas kernels  32.8 us (56%)
  starting transfers between devices  12.6 us (22%)
  waiting for transfers between devices  11.2 us (19%)
  between operations  0.73 us (1%)
    pallas_call x1, Pallas kernels, plan_blocks(): pl.pallas_call(functools.partial(plan_body, layout=layout, row_slots=row_...  14.4 us
    all_to_all x1, waiting for transfers between devices, shards(): lax.all_to_all(outgoing, both, split_axis=0, concat_axis=0, tiled=True)  11.1 us
    pallas_call x1, Pallas kernels, make_kernels(): pl.pallas_call(kernels_body, in_specs=[hbm] * 5, out_specs=pl.BlockSpec(m...  8.73 us
    pallas_call x2, Pallas kernels, grid_part(): pl.pallas_call(functools.partial(grid_body, part=part, first_part=first_p...  8.49 us
    all_to_all x1, starting transfers between devices, shards(): lax.all_to_all(outgoing, both, split_axis=0, concat_axis=0, tiled=True)  7.3 us
    ppermute x3, starting transfers between devices, around(): return lax.ppermute(block, axes, route)  5.25 us
  transfers between devices with their start and end apart: 4, of which 1 were waited for; matrix products, arithmetic and copies ran while one was open for 0% of the time, Pallas kernels for 32%

profile of v6, /device:TPU:0, one launch (start us, length us, event | category | flops | bytes accessed | tf_op | source)
XLA Modules:
  0.0 57.2 jit_solution(13046684518582146679)
XLA Ops:
  0.0 0.0 copy-start
  0.0 0.0 copy-start.1
  0.0 8.7 %make_kernels.1 = bf16[64,64,128]{2,1,0:T(8,128)(2,1)} custom-call(s32[2,32]{1,0:T(2,128)} %bitcast.7, s32[1,32]{1,0:T(1,128)} %count_hbm.1, f32[4]{0:T(128)} %depth_hbm.1, bf16[4,512,512]{2,1,0:T(8,128)(2,1)} %amp_hbm.1, bf16[4,512,512]{2,1,0:T(8,128)(2,1)} %phase_hbm.1), custom_call_target="tpu_custom_call" | custom-call | tf_op jit(solution)/shard_map/make_kernels/pallas_call | solution.py:157
  8.7 7.3 %all-to-all-start = ((bf16[32,2,64,128]{3,2,1,0:T(8,128)(2,1)}), bf16[32,2,64,128]{3,2,1,0:T(8,128)(2,1)S(1)}, u32[]{:S(2)}, u32[]{:S(2)}) async-start(bf16[32,2,64,128]{3,2,1,0:T(8,128)(2,1)} %bitcast.2), calls=%async_computation | async-start | bytes 2097152 | tf_op jit(solution)/shard_map/all_to_all | solution.py:560
  16.7 0.0 copy-done
  16.7 0.0 copy-done.1
  16.7 14.4 %plan_blocks.1 = (s32[659]{0:T(1024)S(4)}, bf16[512,128,128]{2,1,0:T(8,128)(2,1)}, bf16[512,64,128]{2,1,0:T(8,128)(2,1)}) custom-call(s32[384]{0:T(512)S(1)} %copy-done, s32[384]{0:T(512)S(1)} %copy-done.1, s32[1]{0:T(128)S(6)} %copy.19.count_ref, bf16[384,128,128]{2,1,0:T(8,128)(2,1)} %left_hbm.1, bf16[384,64,128]{2,1,0:T(8,128)(2,1)} %right_hbm.1), custom_call_target="tpu_custom_call" | custom-call | tf_op jit(solution)/shard_map/plan_blocks/pallas_call | solution.py:304
  31.1 11.1 %all-to-all-done = bf16[32,2,64,128]{3,2,1,0:T(8,128)(2,1)S(1)} async-done(((bf16[32,2,64,128]{3,2,1,0:T(8,128)(2,1)}), bf16[32,2,64,128]{3,2,1,0:T(8,128)(2,1)S(1)}, u32[]{:S(2)}, u32[]{:S(2)}) %all-to-all-start) | async-done | bytes 1048608 | tf_op jit(solution)/shard_map/all_to_all | solution.py:560
  42.3 4.4 %grid_part.2 = (f32[32,128,256]{2,1,0:T(8,128)S(1)}, bf16[4,32,128,128]{3,2,1,0:T(8,128)(2,1)S(1)}, bf16[4,32,64,128]{3,2,1,0:T(8,128)(2,1)S(1)}, bf16[4,512,256...) custom-call(s32[659]{0:T(1024)S(4)} %get-tuple-element.16.plan_ref, ...), custom_call_target="tpu_custom_call" | custom-call | tf_op jit(solution)/shard_map/grid_part/pallas_call | solution.py:474
  46.7 0.8 %collective-permute-start = (bf16[2,64,512]{2,1,0:T(8,128)(2,1)S(1)}, bf16[2,64,512]{2,1,0:T(8,128)(2,1)S(1)}, u32[]{:S(2)}, u32[]{:S(2)}) collective-permute-start(bf16[2,64,512]{2,1,0:T(8,128)(2,1)S(1)} %get-tuple-element.24), channel_id=1, source_target_pairs={{0,4},{4,8},{8,12},{12,16},{16,20},{20,24},{24,28},{28,0},{1,5},{5... | collective-permute-start | bytes 393224 | tf_op jit(solution)/shard_map/ppermute | solution.py:49
  47.5 0.6 %collective-permute-start.1 = (bf16[256,128]{1,0:T(8,128)(2,1)S(1)}, bf16[256,128]{1,0:T(8,128)(2,1)S(1)}, u32[]{:S(2)}, u32[]{:S(2)}) collective-permute-start(bf16[256,128]{1,0:T(8,128)(2,1)S(1)} %get-tuple-element.25), channel_id=1, source_target_pairs={{0,1},{1,2},{2,3},{3,0},{4,5},{5,6},{6,7},{7,4},{8,9},{9,10},{10,1... | collective-permute-start | bytes 196616 | tf_op jit(solution)/shard_map/ppermute | solution.py:49
  48.1 3.8 %collective-permute-start.2 = (bf16[64,128]{1,0:T(8,128)(2,1)S(1)}, bf16[64,128]{1,0:T(8,128)(2,1)S(1)}, u32[]{:S(2)}, u32[]{:S(2)}) collective-permute-start(bf16[64,128]{1,0:T(8,128)(2,1)S(1)} %get-tuple-element.26), channel_id=1, source_target_pairs={{0,5},{1,6},{2,7},{3,4},{4,9},{5,10},{6,11},{7,8},{8,13},{9,14},{1... | collective-permute-start | bytes 49160 | tf_op jit(solution)/shard_map/ppermute | solution.py:49
  51.9 4.1 %grid_part.3 = (f32[32,128,256]{2,1,0:T(8,128)S(1)}, bf16[4,32,128,128]{3,2,1,0:T(8,128)(2,1)S(1)}, bf16[4,32,64,128]{3,2,1,0:T(8,128)(2,1)S(1)}, bf16[4,512,256]{2,1,0:T(8,128)(2,1)S(1)}) custom-call(s32[659]{0:T(1024)S(4)} %get-tuple-element.16.plan_ref, ...), custom_call_target="tpu_custom_call", output_to_operand_aliasing={{0}: (4, {}), {1}: (5, {}), {2}: (6, {}), {3}: (7, {})} | custom-call | tf_op jit(solution)/shard_map/grid_part/pallas_call | solution.py:474
  56.0 0.0 collective-permute-done.2.corner_ref
  56.1 0.0 collective-permute-done.1.col_ref
  56.1 0.0 collective-permute-done.row_ref
  56.1 1.1 %merge_tile.1 = f32[2,256,512]{2,1,0:T(8,128)} custom-call(f32[32,128,256]{2,1,0:T(8,128)S(1)} %get-tuple-element.23.sums, bf16[2,64,512]{2,1,0:T(8,128)(2,1)S(1)} %collective-permute-done.row_ref, bf16[256,128]{1,0:T(8,128)(2,1)S(1)} %collective-permute-done.1.col_ref, bf16[64,128]{1,0:T(8,128)(2,1)S(1)} %collective-permute-done.2.corner_ref), custom_call_target="tpu_custom_call" | custom-call | tf_op jit(solution)/shard_map/merge_tile/pallas_call | solution.py:527
Async XLA Ops:
  0.0 16.7 %copy-start = (s32[384]{0:T(512)S(1)}, s32[384]{0:T(512)}, u32[]{:S(2)}) copy-start(s32[384]{0:T(512)} %pos_ref.1) | copy-start | bytes 4612
  0.0 16.7 %copy-start.1 = (s32[384]{0:T(512)S(1)}, s32[384]{0:T(512)}, u32[]{:S(2)}) copy-start(s32[384]{0:T(512)} %slot_ref.1) | copy-start | bytes 4612
  8.7 33.5 %all-to-all-start = ((bf16[32,2,64,128]{3,2,1,0:T(8,128)(2,1)}), bf16[32,2,64,128]{3,2,1,0:T(8,128)(2,1)S(1)}, u32[]{:S(2)}, u32[]{:S(2)}) async-start(bf16[32,2,64,128]{3,2,1,0:T(8,128)(2,1)} %bitcast.2), calls=%async_computation | async-start | bytes 2097152 | tf_op jit(solution)/shard_map/all_to_all | solution.py:560
  46.7 9.4 %collective-permute-start = (bf16[2,64,512]{2,1,0:T(8,128)(2,1)S(1)}, bf16[2,64,512]{2,1,0:T(8,128)(2,1)S(1)}, u32[]{:S(2)}, u32[]{:S(2)}) collective-permute-start(bf16[2,64,512]{2,1,0:T(8,128)(2,1)S(1)} %get-tuple-element.24), channel_id=1, source_target_pairs={{0,4},{4,8},{8,12},{12,16},{16,20},{20,24},{24,28},{28,0},{1,5},{5... | collective-permute-start | bytes 393224 | tf_op jit(solution)/shard_map/ppermute | solution.py:49
  47.5 8.6 %collective-permute-start.1 = (bf16[256,128]{1,0:T(8,128)(2,1)S(1)}, bf16[256,128]{1,0:T(8,128)(2,1)S(1)}, u32[]{:S(2)}, u32[]{:S(2)}) collective-permute-start(bf16[256,128]{1,0:T(8,128)(2,1)S(1)} %get-tuple-element.25), channel_id=1, source_target_pairs={{0,1},{1,2},{2,3},{3,0},{4,5},{5,6},{6,7},{7,4},{8,9},{9,10},{10,1... | collective-permute-start | bytes 196616 | tf_op jit(solution)/shard_map/ppermute | solution.py:49
  48.1 7.9 %collective-permute-start.2 = (bf16[64,128]{1,0:T(8,128)(2,1)S(1)}, bf16[64,128]{1,0:T(8,128)(2,1)S(1)}, u32[]{:S(2)}, u32[]{:S(2)}) collective-permute-start(bf16[64,128]{1,0:T(8,128)(2,1)S(1)} %get-tuple-element.26), channel_id=1, source_target_pairs={{0,5},{1,6},{2,7},{3,4},{4,9},{5,10},{6,11},{7,8},{8,13},{9,14},{1... | collective-permute-start | bytes 49160 | tf_op jit(solution)/shard_map/ppermute | solution.py:49

commit v7 on v6

--- a/solution.py
+++ b/solution.py
@@ -12,7 +12,7 @@
 TILE_U = 256
 TILE_V = 512
 QUAD = 4
-UNROLL = 4
+UNROLL = 8
 STEP = 2 * UNROLL
 RING = 4
 LEFT, RIGHT = 0, 1

time: 58.2 us -> 58.1 us (level)
  Pallas kernels: 32.8 us -> 36.7 us
  starting transfers between devices: 12.6 us -> 10.1 us
  waiting for transfers between devices: 11.2 us -> 9.99 us
    all_to_all x1, waiting for transfers between devices: 11.1 us -> 8.04 us  [shards(): lax.all_to_all(outgoing, both, split_axis=0, concat_axis=0, tiled=True)]
    pallas_call x1, Pallas kernels: 14.4 us -> 17.5 us  [plan_blocks(): pl.pallas_call(functools.partial(plan_body, layout=layout, row_slots=row_...]
    ppermute x3, starting transfers between devices: 5.25 us -> 2.77 us  [around(): return lax.ppermute(block, axes, route)]
    ppermute x3, waiting for transfers between devices: 0.01 us -> 1.95 us  [around(): return lax.ppermute(block, axes, route)]
    pallas_call x2, Pallas kernels: 8.49 us -> 9.3 us  [grid_part(): pl.pallas_call(functools.partial(grid_body, part=part, first_part=first_p...]
  transfers between devices with their start and end apart: 4 -> 4, of which waited for: 1 -> 2; matrix products, arithmetic and copies ran while one was open for 0% -> 0% of each run, Pallas kernels for 32% -> 37%
where the time goes in v7:
time: 58.1 us; the launch traced here: 57.5 us
  Pallas kernels  36.7 us (63%)
  starting transfers between devices  10.1 us (17%)
  waiting for transfers between devices  9.99 us (17%)
  between operations  0.71 us (1%)
    pallas_call x1, Pallas kernels, plan_blocks(): pl.pallas_call(functools.partial(plan_body, layout=layout, row_slots=row_...  17.5 us
    pallas_call x2, Pallas kernels, grid_part(): pl.pallas_call(functools.partial(grid_body, part=part, first_part=first_p...  9.3 us
    pallas_call x1, Pallas kernels, make_kernels(): pl.pallas_call(kernels_body, in_specs=[hbm] * 5, out_specs=pl.BlockSpec(m...  8.73 us
    all_to_all x1, waiting for transfers between devices, shards(): lax.all_to_all(outgoing, both, split_axis=0, concat_axis=0, tiled=True)  8.04 us
    all_to_all x1, starting transfers between devices, shards(): lax.all_to_all(outgoing, both, split_axis=0, concat_axis=0, tiled=True)  7.3 us
    ppermute x3, starting transfers between devices, around(): return lax.ppermute(block, axes, route)  2.77 us
    ppermute x3, waiting for transfers between devices, around(): return lax.ppermute(block, axes, route)  1.95 us
  transfers between devices with their start and end apart: 4, of which 2 were waited for; matrix products, arithmetic and copies ran while one was open for 0% of the time, Pallas kernels for 37%

profile of v7, /device:TPU:0, one launch (start us, length us, event | category | flops | bytes accessed | tf_op | source)
XLA Modules:
  0.0 57.5 jit_solution(7879104643014214432)
XLA Ops:
  0.0 0.0 copy-start
  0.0 0.0 copy-start.1
  0.0 8.7 %make_kernels.1 = bf16[64,64,128]{2,1,0:T(8,128)(2,1)} custom-call(s32[2,32]{1,0:T(2,128)} %bitcast.7, s32[1,32]{1,0:T(1,128)} %count_hbm.1, f32[4]{0:T(128)} %depth_hbm.1, bf16[4,512,512]{2,1,0:T(8,128)(2,1)} %amp_hbm.1, bf16[4,512,512]{2,1,0:T(8,128)(2,1)} %phase_hbm.1), custom_call_target="tpu_custom_call" | custom-call | tf_op jit(solution)/shard_map/make_kernels/pallas_call | solution.py:157
  8.7 7.3 %all-to-all-start = ((bf16[32,2,64,128]{3,2,1,0:T(8,128)(2,1)}), bf16[32,2,64,128]{3,2,1,0:T(8,128)(2,1)S(1)}, u32[]{:S(2)}, u32[]{:S(2)}) async-start(bf16[32,2,64,128]{3,2,1,0:T(8,128)(2,1)} %bitcast.2), calls=%async_computation | async-start | bytes 2097152 | tf_op jit(solution)/shard_map/all_to_all | solution.py:560
  16.7 0.0 copy-done
  16.7 0.0 copy-done.1
  16.7 17.5 %plan_blocks.1 = (s32[675]{0:T(1024)S(4)}, bf16[512,128,128]{2,1,0:T(8,128)(2,1)}, bf16[512,64,128]{2,1,0:T(8,128)(2,1)}) custom-call(s32[384]{0:T(512)S(1)} %copy-done, s32[384]{0:T(512)S(1)} %copy-done.1, s32[1]{0:T(128)S(6)} %copy.19.count_ref, bf16[384,128,128]{2,1,0:T(8,128)(2,1)} %left_hbm.1, bf16[384,64,128]{2,1,0:T(8,128)(2,1)} %right_hbm.1), custom_call_target="tpu_custom_call" | custom-call | tf_op jit(solution)/shard_map/plan_blocks/pallas_call | solution.py:304
  34.2 8.0 %all-to-all-done = bf16[32,2,64,128]{3,2,1,0:T(8,128)(2,1)S(1)} async-done(((bf16[32,2,64,128]{3,2,1,0:T(8,128)(2,1)}), bf16[32,2,64,128]{3,2,1,0:T(8,128)(2,1)S(1)}, u32[]{:S(2)}, u32[]{:S(2)}) %all-to-all-start) | async-done | bytes 1048608 | tf_op jit(solution)/shard_map/all_to_all | solution.py:560
  42.3 5.3 %grid_part.2 = (f32[32,128,256]{2,1,0:T(8,128)S(1)}, bf16[4,64,128,128]{3,2,1,0:T(8,128)(2,1)S(1)}, bf16[4,64,64,128]{3,2,1,0:T(8,128)(2,1)S(1)}, bf16[8,512,256...) custom-call(s32[675]{0:T(1024)S(4)} %get-tuple-element.16.plan_ref, ...), custom_call_target="tpu_custom_call" | custom-call | tf_op jit(solution)/shard_map/grid_part/pallas_call | solution.py:474
  47.6 1.5 %collective-permute-start = (bf16[2,64,512]{2,1,0:T(8,128)(2,1)S(1)}, bf16[2,64,512]{2,1,0:T(8,128)(2,1)S(1)}, u32[]{:S(2)}, u32[]{:S(2)}) collective-permute-start(bf16[2,64,512]{2,1,0:T(8,128)(2,1)S(1)} %get-tuple-element.24), channel_id=1, source_target_pairs={{0,4},{4,8},{8,12},{12,16},{16,20},{20,24},{24,28},{28,0},{1,5},{5... | collective-permute-start | bytes 393224 | tf_op jit(solution)/shard_map/ppermute | solution.py:49
  49.2 0.2 collective-permute-start.1
  49.4 1.0 %collective-permute-start.2 = (bf16[64,128]{1,0:T(8,128)(2,1)S(1)}, bf16[64,128]{1,0:T(8,128)(2,1)S(1)}, u32[]{:S(2)}, u32[]{:S(2)}) collective-permute-start(bf16[64,128]{1,0:T(8,128)(2,1)S(1)} %get-tuple-element.26), channel_id=1, source_target_pairs={{0,5},{1,6},{2,7},{3,4},{4,9},{5,10},{6,11},{7,8},{8,13},{9,14},{1... | collective-permute-start | bytes 49160 | tf_op jit(solution)/shard_map/ppermute | solution.py:49
  50.4 4.0 %grid_part.3 = (f32[32,128,256]{2,1,0:T(8,128)S(1)}, bf16[4,64,128,128]{3,2,1,0:T(8,128)(2,1)S(1)}, bf16[4,64,64,128]{3,2,1,0:T(8,128)(2,1)S(1)}, bf16[8,512,256]{2,1,0:T(8,128)(2,1)S(1)}) custom-call(s32[675]{0:T(1024)S(4)} %get-tuple-element.16.plan_ref, ...), custom_call_target="tpu_custom_call", output_to_operand_aliasing={{0}: (4, {}), {1}: (5, {}), {2}: (6, {}), {3}: (7, {})} | custom-call | tf_op jit(solution)/shard_map/grid_part/pallas_call | solution.py:474
  54.4 1.9 %collective-permute-done.2.corner_ref = bf16[64,128]{1,0:T(8,128)(2,1)S(1)} collective-permute-done((bf16[64,128]{1,0:T(8,128)(2,1)S(1)}, bf16[64,128]{1,0:T(8,128)(2,1)S(1)}, u32[]{:S(2)}, u32[]{:S(2)}) %collective-permute-start.2) | collective-permute-done | bytes 16416 | tf_op jit(solution)/shard_map/ppermute | solution.py:49
  56.3 0.0 collective-permute-done.1.col_ref
  56.3 0.0 collective-permute-done.row_ref
  56.3 1.1 %merge_tile.1 = f32[2,256,512]{2,1,0:T(8,128)} custom-call(f32[32,128,256]{2,1,0:T(8,128)S(1)} %get-tuple-element.23.sums, bf16[2,64,512]{2,1,0:T(8,128)(2,1)S(1)} %collective-permute-done.row_ref, bf16[256,128]{1,0:T(8,128)(2,1)S(1)} %collective-permute-done.1.col_ref, bf16[64,128]{1,0:T(8,128)(2,1)S(1)} %collective-permute-done.2.corner_ref), custom_call_target="tpu_custom_call" | custom-call | tf_op jit(solution)/shard_map/merge_tile/pallas_call | solution.py:527
Async XLA Ops:
  0.0 16.7 %copy-start = (s32[384]{0:T(512)S(1)}, s32[384]{0:T(512)}, u32[]{:S(2)}) copy-start(s32[384]{0:T(512)} %pos_ref.1) | copy-start | bytes 4612
  0.0 16.7 %copy-start.1 = (s32[384]{0:T(512)S(1)}, s32[384]{0:T(512)}, u32[]{:S(2)}) copy-start(s32[384]{0:T(512)} %slot_ref.1) | copy-start | bytes 4612
  8.7 33.5 %all-to-all-start = ((bf16[32,2,64,128]{3,2,1,0:T(8,128)(2,1)}), bf16[32,2,64,128]{3,2,1,0:T(8,128)(2,1)S(1)}, u32[]{:S(2)}, u32[]{:S(2)}) async-start(bf16[32,2,64,128]{3,2,1,0:T(8,128)(2,1)} %bitcast.2), calls=%async_computation | async-start | bytes 2097152 | tf_op jit(solution)/shard_map/all_to_all | solution.py:560
  47.6 8.7 %collective-permute-start = (bf16[2,64,512]{2,1,0:T(8,128)(2,1)S(1)}, bf16[2,64,512]{2,1,0:T(8,128)(2,1)S(1)}, u32[]{:S(2)}, u32[]{:S(2)}) collective-permute-start(bf16[2,64,512]{2,1,0:T(8,128)(2,1)S(1)} %get-tuple-element.24), channel_id=1, source_target_pairs={{0,4},{4,8},{8,12},{12,16},{16,20},{20,24},{24,28},{28,0},{1,5},{5... | collective-permute-start | bytes 393224 | tf_op jit(solution)/shard_map/ppermute | solution.py:49
  49.2 7.2 %collective-permute-start.1 = (bf16[256,128]{1,0:T(8,128)(2,1)S(1)}, bf16[256,128]{1,0:T(8,128)(2,1)S(1)}, u32[]{:S(2)}, u32[]{:S(2)}) collective-permute-start(bf16[256,128]{1,0:T(8,128)(2,1)S(1)} %get-tuple-element.25), channel_id=1, source_target_pairs={{0,1},{1,2},{2,3},{3,0},{4,5},{5,6},{6,7},{7,4},{8,9},{9,10},{10,1... | collective-permute-start | bytes 196616 | tf_op jit(solution)/shard_map/ppermute | solution.py:49
  49.4 6.9 %collective-permute-start.2 = (bf16[64,128]{1,0:T(8,128)(2,1)S(1)}, bf16[64,128]{1,0:T(8,128)(2,1)S(1)}, u32[]{:S(2)}, u32[]{:S(2)}) collective-permute-start(bf16[64,128]{1,0:T(8,128)(2,1)S(1)} %get-tuple-element.26), channel_id=1, source_target_pairs={{0,5},{1,6},{2,7},{3,4},{4,9},{5,10},{6,11},{7,8},{8,13},{9,14},{1... | collective-permute-start | bytes 49160 | tf_op jit(solution)/shard_map/ppermute | solution.py:49

commit v8 on v7

--- a/solution.py
+++ b/solution.py
@@ -142,7 +142,7 @@
 
     capacity, tiles = chosen_list.shape
 
-    @pl.loop(0, tiles)
+    @pl.loop(0, tiles, unroll=8)
     def _(t):
         for c in range(capacity):
             chosen = made[chosen_list[c, t]]
@@ -373,7 +373,6 @@
 
     if first_part:
         start(0, RIGHT)
-        start(1, RIGHT)
         start(0, LEFT)
 
         @pl.loop(0, sums.shape[0])
@@ -405,6 +404,7 @@
 
     if first_part:
         wait(0, RIGHT)
+        start(1, RIGHT)
         start(1, LEFT)
         for u in range(UNROLL):
             first(0, 0, u, mixed[0], u)

time: 58.1 us -> 58.5 us (level)
  Pallas kernels: 36.7 us -> 33.4 us
  waiting for transfers between devices: 9.99 us -> 12.8 us
  starting transfers between devices: 10.1 us -> 11.4 us
    all_to_all x1, waiting for transfers between devices: 8.04 us -> 9.96 us  [shards(): lax.all_to_all(outgoing, both, split_axis=0, concat_axis=0, tiled=True)]
    pallas_call x1, Pallas kernels: 17.5 us -> 15.6 us  [plan_blocks(): pl.pallas_call(functools.partial(plan_body, layout=layout, row_slots=row_...]
    ppermute x3, starting transfers between devices: 2.77 us -> 4.1 us  [around(): return lax.ppermute(block, axes, route)]
    pallas_call x2, Pallas kernels: 9.3 us -> 8.09 us  [grid_part(): pl.pallas_call(functools.partial(grid_body, part=part, first_part=first_p...]
    ppermute x3, waiting for transfers between devices: 1.95 us -> 2.82 us  [around(): return lax.ppermute(block, axes, route)]
  transfers between devices with their start and end apart: 4 -> 4, of which waited for: 2 -> 2; matrix products, arithmetic and copies ran while one was open for 0% -> 0% of each run, Pallas kernels for 37% -> 31%
where the time goes in v8:
time: 58.5 us; the launch traced here: 58.3 us
  Pallas kernels  33.4 us (57%)
  waiting for transfers between devices  12.8 us (22%)
  starting transfers between devices  11.4 us (19%)
  between operations  0.71 us (1%)
    pallas_call x1, Pallas kernels, plan_blocks(): pl.pallas_call(functools.partial(plan_body, layout=layout, row_slots=row_...  15.6 us
    all_to_all x1, waiting for transfers between devices, shards(): lax.all_to_all(outgoing, both, split_axis=0, concat_axis=0, tiled=True)  9.96 us
    pallas_call x1, Pallas kernels, make_kernels(): pl.pallas_call(kernels_body, in_specs=[hbm] * 5, out_specs=pl.BlockSpec(m...  8.6 us
    pallas_call x2, Pallas kernels, grid_part(): pl.pallas_call(functools.partial(grid_body, part=part, first_part=first_p...  8.09 us
    all_to_all x1, starting transfers between devices, shards(): lax.all_to_all(outgoing, both, split_axis=0, concat_axis=0, tiled=True)  7.3 us
    ppermute x3, starting transfers between devices, around(): return lax.ppermute(block, axes, route)  4.1 us
    ppermute x3, waiting for transfers between devices, around(): return lax.ppermute(block, axes, route)  2.82 us
  transfers between devices with their start and end apart: 4, of which 2 were waited for; matrix products, arithmetic and copies ran while one was open for 0% of the time, Pallas kernels for 31%

profile of v8, /device:TPU:0, one launch (start us, length us, event | category | flops | bytes accessed | tf_op | source)
XLA Modules:
  0.0 58.3 jit_solution(14823111759249762644)
XLA Ops:
  0.0 0.0 copy-start
  0.0 0.0 copy-start.1
  0.0 8.6 %make_kernels.1 = bf16[64,64,128]{2,1,0:T(8,128)(2,1)} custom-call(s32[2,32]{1,0:T(2,128)} %bitcast.7, s32[1,32]{1,0:T(1,128)} %count_hbm.1, f32[4]{0:T(128)} %depth_hbm.1, bf16[4,512,512]{2,1,0:T(8,128)(2,1)} %amp_hbm.1, bf16[4,512,512]{2,1,0:T(8,128)(2,1)} %phase_hbm.1), custom_call_target="tpu_custom_call" | custom-call | tf_op jit(solution)/shard_map/make_kernels/pallas_call | solution.py:157
  8.6 7.3 %all-to-all-start = ((bf16[32,2,64,128]{3,2,1,0:T(8,128)(2,1)}), bf16[32,2,64,128]{3,2,1,0:T(8,128)(2,1)S(1)}, u32[]{:S(2)}, u32[]{:S(2)}) async-start(bf16[32,2,64,128]{3,2,1,0:T(8,128)(2,1)} %bitcast.2), calls=%async_computation | async-start | bytes 2097152 | tf_op jit(solution)/shard_map/all_to_all | solution.py:560
  16.6 0.0 copy-done
  16.6 0.0 copy-done.1
  16.6 15.6 %plan_blocks.1 = (s32[675]{0:T(1024)S(4)}, bf16[512,128,128]{2,1,0:T(8,128)(2,1)}, bf16[512,64,128]{2,1,0:T(8,128)(2,1)}) custom-call(s32[384]{0:T(512)S(1)} %copy-done, s32[384]{0:T(512)S(1)} %copy-done.1, s32[1]{0:T(128)S(6)} %copy.19.count_ref, bf16[384,128,128]{2,1,0:T(8,128)(2,1)} %left_hbm.1, bf16[384,64,128]{2,1,0:T(8,128)(2,1)} %right_hbm.1), custom_call_target="tpu_custom_call" | custom-call | tf_op jit(solution)/shard_map/plan_blocks/pallas_call | solution.py:304
  32.2 10.0 %all-to-all-done = bf16[32,2,64,128]{3,2,1,0:T(8,128)(2,1)S(1)} async-done(((bf16[32,2,64,128]{3,2,1,0:T(8,128)(2,1)}), bf16[32,2,64,128]{3,2,1,0:T(8,128)(2,1)S(1)}, u32[]{:S(2)}, u32[]{:S(2)}) %all-to-all-start) | async-done | bytes 1048608 | tf_op jit(solution)/shard_map/all_to_all | solution.py:560
  42.2 5.4 %grid_part.2 = (f32[32,128,256]{2,1,0:T(8,128)S(1)}, bf16[4,64,128,128]{3,2,1,0:T(8,128)(2,1)S(1)}, bf16[4,64,64,128]{3,2,1,0:T(8,128)(2,1)S(1)}, bf16[8,512,256...) custom-call(s32[675]{0:T(1024)S(4)} %get-tuple-element.16.plan_ref, ...), custom_call_target="tpu_custom_call" | custom-call | tf_op jit(solution)/shard_map/grid_part/pallas_call | solution.py:474
  47.6 2.8 %collective-permute-start = (bf16[2,64,512]{2,1,0:T(8,128)(2,1)S(1)}, bf16[2,64,512]{2,1,0:T(8,128)(2,1)S(1)}, u32[]{:S(2)}, u32[]{:S(2)}) collective-permute-start(bf16[2,64,512]{2,1,0:T(8,128)(2,1)S(1)} %get-tuple-element.24), channel_id=1, source_target_pairs={{0,4},{4,8},{8,12},{12,16},{16,20},{20,24},{24,28},{28,0},{1,5},{5... | collective-permute-start | bytes 393224 | tf_op jit(solution)/shard_map/ppermute | solution.py:49
  50.4 0.0 collective-permute-start.1
  50.4 1.3 %collective-permute-start.2 = (bf16[64,128]{1,0:T(8,128)(2,1)S(1)}, bf16[64,128]{1,0:T(8,128)(2,1)S(1)}, u32[]{:S(2)}, u32[]{:S(2)}) collective-permute-start(bf16[64,128]{1,0:T(8,128)(2,1)S(1)} %get-tuple-element.26), channel_id=1, source_target_pairs={{0,5},{1,6},{2,7},{3,4},{4,9},{5,10},{6,11},{7,8},{8,13},{9,14},{1... | collective-permute-start | bytes 49160 | tf_op jit(solution)/shard_map/ppermute | solution.py:49
  51.7 2.7 %grid_part.3 = (f32[32,128,256]{2,1,0:T(8,128)S(1)}, bf16[4,64,128,128]{3,2,1,0:T(8,128)(2,1)S(1)}, bf16[4,64,64,128]{3,2,1,0:T(8,128)(2,1)S(1)}, bf16[8,512,256]{2,1,0:T(8,128)(2,1)S(1)}) custom-call(s32[675]{0:T(1024)S(4)} %get-tuple-element.16.plan_ref, ...), custom_call_target="tpu_custom_call", output_to_operand_aliasing={{0}: (4, {}), {1}: (5, {}), {2}: (6, {}), {3}: (7, {})} | custom-call | tf_op jit(solution)/shard_map/grid_part/pallas_call | solution.py:474
  54.4 2.8 %collective-permute-done.2.corner_ref = bf16[64,128]{1,0:T(8,128)(2,1)S(1)} collective-permute-done((bf16[64,128]{1,0:T(8,128)(2,1)S(1)}, bf16[64,128]{1,0:T(8,128)(2,1)S(1)}, u32[]{:S(2)}, u32[]{:S(2)}) %collective-permute-start.2) | collective-permute-done | bytes 16416 | tf_op jit(solution)/shard_map/ppermute | solution.py:49
  57.2 0.0 collective-permute-done.1.col_ref
  57.2 0.0 collective-permute-done.row_ref
  57.2 1.1 %merge_tile.1 = f32[2,256,512]{2,1,0:T(8,128)} custom-call(f32[32,128,256]{2,1,0:T(8,128)S(1)} %get-tuple-element.23.sums, bf16[2,64,512]{2,1,0:T(8,128)(2,1)S(1)} %collective-permute-done.row_ref, bf16[256,128]{1,0:T(8,128)(2,1)S(1)} %collective-permute-done.1.col_ref, bf16[64,128]{1,0:T(8,128)(2,1)S(1)} %collective-permute-done.2.corner_ref), custom_call_target="tpu_custom_call" | custom-call | tf_op jit(solution)/shard_map/merge_tile/pallas_call | solution.py:527
Async XLA Ops:
  0.0 16.6 %copy-start = (s32[384]{0:T(512)S(1)}, s32[384]{0:T(512)}, u32[]{:S(2)}) copy-start(s32[384]{0:T(512)} %pos_ref.1) | copy-start | bytes 4612
  0.0 16.6 %copy-start.1 = (s32[384]{0:T(512)S(1)}, s32[384]{0:T(512)}, u32[]{:S(2)}) copy-start(s32[384]{0:T(512)} %slot_ref.1) | copy-start | bytes 4612
  8.6 33.5 %all-to-all-start = ((bf16[32,2,64,128]{3,2,1,0:T(8,128)(2,1)}), bf16[32,2,64,128]{3,2,1,0:T(8,128)(2,1)S(1)}, u32[]{:S(2)}, u32[]{:S(2)}) async-start(bf16[32,2,64,128]{3,2,1,0:T(8,128)(2,1)} %bitcast.2), calls=%async_computation | async-start | bytes 2097152 | tf_op jit(solution)/shard_map/all_to_all | solution.py:560
  47.6 9.6 %collective-permute-start = (bf16[2,64,512]{2,1,0:T(8,128)(2,1)S(1)}, bf16[2,64,512]{2,1,0:T(8,128)(2,1)S(1)}, u32[]{:S(2)}, u32[]{:S(2)}) collective-permute-start(bf16[2,64,512]{2,1,0:T(8,128)(2,1)S(1)} %get-tuple-element.24), channel_id=1, source_target_pairs={{0,4},{4,8},{8,12},{12,16},{16,20},{20,24},{24,28},{28,0},{1,5},{5... | collective-permute-start | bytes 393224 | tf_op jit(solution)/shard_map/ppermute | solution.py:49
  50.4 6.8 %collective-permute-start.1 = (bf16[256,128]{1,0:T(8,128)(2,1)S(1)}, bf16[256,128]{1,0:T(8,128)(2,1)S(1)}, u32[]{:S(2)}, u32[]{:S(2)}) collective-permute-start(bf16[256,128]{1,0:T(8,128)(2,1)S(1)} %get-tuple-element.25), channel_id=1, source_target_pairs={{0,1},{1,2},{2,3},{3,0},{4,5},{5,6},{6,7},{7,4},{8,9},{9,10},{10,1... | collective-permute-start | bytes 196616 | tf_op jit(solution)/shard_map/ppermute | solution.py:49
  50.4 6.8 %collective-permute-start.2 = (bf16[64,128]{1,0:T(8,128)(2,1)S(1)}, bf16[64,128]{1,0:T(8,128)(2,1)S(1)}, u32[]{:S(2)}, u32[]{:S(2)}) collective-permute-start(bf16[64,128]{1,0:T(8,128)(2,1)S(1)} %get-tuple-element.26), channel_id=1, source_target_pairs={{0,5},{1,6},{2,7},{3,4},{4,9},{5,10},{6,11},{7,8},{8,13},{9,14},{1... | collective-permute-start | bytes 49160 | tf_op jit(solution)/shard_map/ppermute | solution.py:49

commit v9 on v8

--- a/solution.py
+++ b/solution.py
@@ -81,14 +81,19 @@
     for copy in small:
         copy.start()
 
-    def bulk(s):
+    halfway = size // 2
+    row_halves = (slice(0, halfway), slice(halfway, size))
+
+    def bulk(s, h):
+        rows = row_halves[h]
         return [
-            pltpu.make_async_copy(amp_hbm.at[s], amp.at[s], bulk_sems.at[0, s]),
-            pltpu.make_async_copy(phase_hbm.at[s], phase.at[s], bulk_sems.at[1, s]),
+            pltpu.make_async_copy(amp_hbm.at[s, rows], amp.at[s, rows], bulk_sems.at[h, s]),
+            pltpu.make_async_copy(phase_hbm.at[s, rows], phase.at[s, rows], bulk_sems.at[2 + h, s]),
         ]
 
-    for copy in bulk(0):
-        copy.start()
+    for h in range(2):
+        for copy in bulk(0, h):
+            copy.start()
 
     frequency = lax.broadcasted_iota(jnp.int32, (kernel_size, size), 0) - kernel_size // 2
     cells = lax.broadcasted_iota(jnp.int32, (kernel_size, size), 1)
@@ -101,8 +106,9 @@
     for copy in small:
         copy.wait()
     for s in range(1, screens):
-        for copy in bulk(s):
-            copy.start()
+        for h in range(2):
+            for copy in bulk(s, h):
+                copy.start()
     for p in range(planes):
         turns = depth[p] * square
         real_e, imag_e = cos_sin((2.0 * math.pi) * (turns - jnp.round(turns)))
@@ -117,12 +123,13 @@
 
     @pl.loop(0, screens)
     def _(s):
-        for copy in bulk(s):
-            copy.wait()
-        magnitude = amp[s].astype(jnp.float32)
-        real_e, imag_e = cos_sin(phase[s].astype(jnp.float32))
-        screen[:size, :] = (magnitude * real_e).astype(jnp.bfloat16)
-        screen[size:, :] = (magnitude * imag_e).astype(jnp.bfloat16)
+        for h, rows in enumerate(row_halves):
+            for copy in bulk(s, h):
+                copy.wait()
+            magnitude = amp[s, rows].astype(jnp.float32)
+            real_e, imag_e = cos_sin(phase[s, rows].astype(jnp.float32))
+            screen[rows, :] = (magnitude * real_e).astype(jnp.bfloat16)
+            screen[slice(size + rows.start, size + rows.stop), :] = (magnitude * imag_e).astype(jnp.bfloat16)
         product = jnp.dot(table[...], screen[...], preferred_element_type=jnp.float32).astype(jnp.bfloat16)
         for p in range(planes):
             base = p * 2 * kernel_size
@@ -170,7 +177,7 @@
             pltpu.VMEM((screens, planes, kernel_size, 2 * size), jnp.bfloat16),
             pltpu.VMEM((screens * planes, kernel_size, 2 * kernel_size), jnp.bfloat16),
             pltpu.SemaphoreType.DMA((3,)),
-            pltpu.SemaphoreType.DMA((2, screens)),
+            pltpu.SemaphoreType.DMA((4, screens)),
         ],
         compiler_params=pltpu.CompilerParams(vmem_limit_bytes=32 * 2**20),
         name="make_kernels",
@@ -373,6 +380,7 @@
 
     if first_part:
         start(0, RIGHT)
+        start(1, RIGHT)
         start(0, LEFT)
 
         @pl.loop(0, sums.shape[0])
@@ -404,7 +412,6 @@
 
     if first_part:
         wait(0, RIGHT)
-        start(1, RIGHT)
         start(1, LEFT)
         for u in range(UNROLL):
             first(0, 0, u, mixed[0], u)

time: 58.5 us -> 60.2 us (1.029); the launches traced: 58.3 us -> 59.3 us
  Pallas kernels: 33.4 us -> 38.4 us
  waiting for transfers between devices: 12.8 us -> 8.85 us
    all_to_all x1, waiting for transfers between devices: 9.96 us -> 7.92 us  [shards(): lax.all_to_all(outgoing, both, split_axis=0, concat_axis=0, tiled=True)]
    pallas_call x1, Pallas kernels: 15.6 us -> 17.6 us  [plan_blocks(): pl.pallas_call(functools.partial(plan_body, layout=layout, row_slots=row_...]
    ppermute x3, waiting for transfers between devices: 2.82 us -> 0.94 us  [around(): return lax.ppermute(block, axes, route)]
    pallas_call x1, Pallas kernels: 8.6 us -> 10.3 us  [make_kernels(): pl.pallas_call(kernels_body, in_specs=[hbm] * 5, out_specs=pl.BlockSpec(m...]
    pallas_call x2, Pallas kernels: 8.09 us -> 9.3 us  [grid_part(): pl.pallas_call(functools.partial(grid_body, part=part, first_part=first_p...]
  transfers between devices with their start and end apart: 4 -> 4, of which waited for: 2 -> 2; matrix products, arithmetic and copies ran while one was open for 0% -> 0% of each run, Pallas kernels for 31% -> 36%
where the time goes in v9:
time: 60.2 us; the launch traced here: 59.3 us
  Pallas kernels  38.4 us (64%)
  starting transfers between devices  11.3 us (19%)
  waiting for transfers between devices  8.85 us (15%)
  between operations  0.71 us (1%)
    pallas_call x1, Pallas kernels, plan_blocks(): pl.pallas_call(functools.partial(plan_body, layout=layout, row_slots=row_...  17.6 us
    pallas_call x1, Pallas kernels, make_kernels(): pl.pallas_call(kernels_body, in_specs=[hbm] * 5, out_specs=pl.BlockSpec(m...  10.3 us
    pallas_call x2, Pallas kernels, grid_part(): pl.pallas_call(functools.partial(grid_body, part=part, first_part=first_p...  9.3 us
    all_to_all x1, waiting for transfers between devices, shards(): lax.all_to_all(outgoing, both, split_axis=0, concat_axis=0, tiled=True)  7.92 us
    all_to_all x1, starting transfers between devices, shards(): lax.all_to_all(outgoing, both, split_axis=0, concat_axis=0, tiled=True)  7.3 us
    ppermute x3, starting transfers between devices, around(): return lax.ppermute(block, axes, route)  4 us
  transfers between devices with their start and end apart: 4, of which 2 were waited for; matrix products, arithmetic and copies ran while one was open for 0% of the time, Pallas kernels for 36%

profile of v9, /device:TPU:0, one launch (start us, length us, event | category | flops | bytes accessed | tf_op | source)
XLA Modules:
  0.0 59.3 jit_solution(15167508036131556939)
XLA Ops:
  0.0 0.0 copy-start
  0.0 0.0 copy-start.1
  0.0 10.3 %make_kernels.1 = bf16[64,64,128]{2,1,0:T(8,128)(2,1)} custom-call(s32[2,32]{1,0:T(2,128)} %bitcast.7, s32[1,32]{1,0:T(1,128)} %count_hbm.1, f32[4]{0:T(128)} %depth_hbm.1, bf16[4,512,512]{2,1,0:T(8,128)(2,1)} %amp_hbm.1, bf16[4,512,512]{2,1,0:T(8,128)(2,1)} %phase_hbm.1), custom_call_target="tpu_custom_call" | custom-call | tf_op jit(solution)/shard_map/make_kernels/pallas_call | solution.py:164
  10.3 7.3 %all-to-all-start = ((bf16[32,2,64,128]{3,2,1,0:T(8,128)(2,1)}), bf16[32,2,64,128]{3,2,1,0:T(8,128)(2,1)S(1)}, u32[]{:S(2)}, u32[]{:S(2)}) async-start(bf16[32,2,64,128]{3,2,1,0:T(8,128)(2,1)} %bitcast.2), calls=%async_computation | async-start | bytes 2097152 | tf_op jit(solution)/shard_map/all_to_all | solution.py:567
  18.3 0.0 copy-done
  18.3 0.0 copy-done.1
  18.3 17.6 %plan_blocks.1 = (s32[675]{0:T(1024)S(4)}, bf16[512,128,128]{2,1,0:T(8,128)(2,1)}, bf16[512,64,128]{2,1,0:T(8,128)(2,1)}) custom-call(s32[384]{0:T(512)S(1)} %copy-done, s32[384]{0:T(512)S(1)} %copy-done.1, s32[1]{0:T(128)S(6)} %copy.19.count_ref, bf16[384,128,128]{2,1,0:T(8,128)(2,1)} %left_hbm.1, bf16[384,64,128]{2,1,0:T(8,128)(2,1)} %right_hbm.1), custom_call_target="tpu_custom_call" | custom-call | tf_op jit(solution)/shard_map/plan_blocks/pallas_call | solution.py:311
  36.0 7.9 %all-to-all-done = bf16[32,2,64,128]{3,2,1,0:T(8,128)(2,1)S(1)} async-done(((bf16[32,2,64,128]{3,2,1,0:T(8,128)(2,1)}), bf16[32,2,64,128]{3,2,1,0:T(8,128)(2,1)S(1)}, u32[]{:S(2)}, u32[]{:S(2)}) %all-to-all-start) | async-done | bytes 1048608 | tf_op jit(solution)/shard_map/all_to_all | solution.py:567
  43.9 5.3 %grid_part.2 = (f32[32,128,256]{2,1,0:T(8,128)S(1)}, bf16[4,64,128,128]{3,2,1,0:T(8,128)(2,1)S(1)}, bf16[4,64,64,128]{3,2,1,0:T(8,128)(2,1)S(1)}, bf16[8,512,256...) custom-call(s32[675]{0:T(1024)S(4)} %get-tuple-element.16.plan_ref, ...), custom_call_target="tpu_custom_call" | custom-call | tf_op jit(solution)/shard_map/grid_part/pallas_call | solution.py:481
  49.2 1.5 %collective-permute-start = (bf16[2,64,512]{2,1,0:T(8,128)(2,1)S(1)}, bf16[2,64,512]{2,1,0:T(8,128)(2,1)S(1)}, u32[]{:S(2)}, u32[]{:S(2)}) collective-permute-start(bf16[2,64,512]{2,1,0:T(8,128)(2,1)S(1)} %get-tuple-element.24), channel_id=1, source_target_pairs={{0,4},{4,8},{8,12},{12,16},{16,20},{20,24},{24,28},{28,0},{1,5},{5... | collective-permute-start | bytes 393224 | tf_op jit(solution)/shard_map/ppermute | solution.py:49
  50.7 0.0 collective-permute-start.1
  50.7 2.5 %collective-permute-start.2 = (bf16[64,128]{1,0:T(8,128)(2,1)S(1)}, bf16[64,128]{1,0:T(8,128)(2,1)S(1)}, u32[]{:S(2)}, u32[]{:S(2)}) collective-permute-start(bf16[64,128]{1,0:T(8,128)(2,1)S(1)} %get-tuple-element.26), channel_id=1, source_target_pairs={{0,5},{1,6},{2,7},{3,4},{4,9},{5,10},{6,11},{7,8},{8,13},{9,14},{1... | collective-permute-start | bytes 49160 | tf_op jit(solution)/shard_map/ppermute | solution.py:49
  53.2 4.0 %grid_part.3 = (f32[32,128,256]{2,1,0:T(8,128)S(1)}, bf16[4,64,128,128]{3,2,1,0:T(8,128)(2,1)S(1)}, bf16[4,64,64,128]{3,2,1,0:T(8,128)(2,1)S(1)}, bf16[8,512,256]{2,1,0:T(8,128)(2,1)S(1)}) custom-call(s32[675]{0:T(1024)S(4)} %get-tuple-element.16.plan_ref, ...), custom_call_target="tpu_custom_call", output_to_operand_aliasing={{0}: (4, {}), {1}: (5, {}), {2}: (6, {}), {3}: (7, {})} | custom-call | tf_op jit(solution)/shard_map/grid_part/pallas_call | solution.py:481
  57.2 0.9 %collective-permute-done.2.corner_ref = bf16[64,128]{1,0:T(8,128)(2,1)S(1)} collective-permute-done((bf16[64,128]{1,0:T(8,128)(2,1)S(1)}, bf16[64,128]{1,0:T(8,128)(2,1)S(1)}, u32[]{:S(2)}, u32[]{:S(2)}) %collective-permute-start.2) | collective-permute-done | bytes 16416 | tf_op jit(solution)/shard_map/ppermute | solution.py:49
  58.1 0.0 collective-permute-done.1.col_ref
  58.1 0.0 collective-permute-done.row_ref
  58.1 1.1 %merge_tile.1 = f32[2,256,512]{2,1,0:T(8,128)} custom-call(f32[32,128,256]{2,1,0:T(8,128)S(1)} %get-tuple-element.23.sums, bf16[2,64,512]{2,1,0:T(8,128)(2,1)S(1)} %collective-permute-done.row_ref, bf16[256,128]{1,0:T(8,128)(2,1)S(1)} %collective-permute-done.1.col_ref, bf16[64,128]{1,0:T(8,128)(2,1)S(1)} %collective-permute-done.2.corner_ref), custom_call_target="tpu_custom_call" | custom-call | tf_op jit(solution)/shard_map/merge_tile/pallas_call | solution.py:534
Async XLA Ops:
  0.0 18.3 %copy-start = (s32[384]{0:T(512)S(1)}, s32[384]{0:T(512)}, u32[]{:S(2)}) copy-start(s32[384]{0:T(512)} %pos_ref.1) | copy-start | bytes 4612
  0.0 18.3 %copy-start.1 = (s32[384]{0:T(512)S(1)}, s32[384]{0:T(512)}, u32[]{:S(2)}) copy-start(s32[384]{0:T(512)} %slot_ref.1) | copy-start | bytes 4612
  10.3 33.5 %all-to-all-start = ((bf16[32,2,64,128]{3,2,1,0:T(8,128)(2,1)}), bf16[32,2,64,128]{3,2,1,0:T(8,128)(2,1)S(1)}, u32[]{:S(2)}, u32[]{:S(2)}) async-start(bf16[32,2,64,128]{3,2,1,0:T(8,128)(2,1)} %bitcast.2), calls=%async_computation | async-start | bytes 2097152 | tf_op jit(solution)/shard_map/all_to_all | solution.py:567
  49.2 8.9 %collective-permute-start = (bf16[2,64,512]{2,1,0:T(8,128)(2,1)S(1)}, bf16[2,64,512]{2,1,0:T(8,128)(2,1)S(1)}, u32[]{:S(2)}, u32[]{:S(2)}) collective-permute-start(bf16[2,64,512]{2,1,0:T(8,128)(2,1)S(1)} %get-tuple-element.24), channel_id=1, source_target_pairs={{0,4},{4,8},{8,12},{12,16},{16,20},{20,24},{24,28},{28,0},{1,5},{5... | collective-permute-start | bytes 393224 | tf_op jit(solution)/shard_map/ppermute | solution.py:49
  50.7 7.4 %collective-permute-start.1 = (bf16[256,128]{1,0:T(8,128)(2,1)S(1)}, bf16[256,128]{1,0:T(8,128)(2,1)S(1)}, u32[]{:S(2)}, u32[]{:S(2)}) collective-permute-start(bf16[256,128]{1,0:T(8,128)(2,1)S(1)} %get-tuple-element.25), channel_id=1, source_target_pairs={{0,1},{1,2},{2,3},{3,0},{4,5},{5,6},{6,7},{7,4},{8,9},{9,10},{10,1... | collective-permute-start | bytes 196616 | tf_op jit(solution)/shard_map/ppermute | solution.py:49
  50.7 7.4 %collective-permute-start.2 = (bf16[64,128]{1,0:T(8,128)(2,1)S(1)}, bf16[64,128]{1,0:T(8,128)(2,1)S(1)}, u32[]{:S(2)}, u32[]{:S(2)}) collective-permute-start(bf16[64,128]{1,0:T(8,128)(2,1)S(1)} %get-tuple-element.26), channel_id=1, source_target_pairs={{0,5},{1,6},{2,7},{3,4},{4,9},{5,10},{6,11},{7,8},{8,13},{9,14},{1... | collective-permute-start | bytes 49160 | tf_op jit(solution)/shard_map/ppermute | solution.py:49

commit v10 on v8

--- a/solution.py
+++ b/solution.py
@@ -373,6 +373,7 @@
 
     if first_part:
         start(0, RIGHT)
+        start(1, RIGHT)
         start(0, LEFT)
 
         @pl.loop(0, sums.shape[0])
@@ -404,7 +405,6 @@
 
     if first_part:
         wait(0, RIGHT)
-        start(1, RIGHT)
         start(1, LEFT)
         for u in range(UNROLL):
             first(0, 0, u, mixed[0], u)

time: 58.5 us -> 58.3 us (level)
  waiting for transfers between devices: 12.8 us -> 5.09 us
  Pallas kernels: 33.4 us -> 40.8 us
    all_to_all x1, waiting for transfers between devices: 9.96 us -> 5.09 us  [shards(): lax.all_to_all(outgoing, both, split_axis=0, concat_axis=0, tiled=True)]
    pallas_call x1, Pallas kernels: 15.6 us -> 20.5 us  [plan_blocks(): pl.pallas_call(functools.partial(plan_body, layout=layout, row_slots=row_...]
    ppermute x3, waiting for transfers between devices: 2.82 us -> 0.01 us  [around(): return lax.ppermute(block, axes, route)]
    pallas_call x2, Pallas kernels: 8.09 us -> 10.6 us  [grid_part(): pl.pallas_call(functools.partial(grid_body, part=part, first_part=first_p...]
  transfers between devices with their start and end apart: 4 -> 4, of which waited for: 2 -> 1; matrix products, arithmetic and copies ran while one was open for 0% -> 0% of each run, Pallas kernels for 31% -> 44%
where the time goes in v10:
time: 58.3 us; the launch traced here: 58 us
  Pallas kernels  40.8 us (70%)
  starting transfers between devices  11.3 us (19%)
  waiting for transfers between devices  5.09 us (9%)
  between operations  0.73 us (1%)
    pallas_call x1, Pallas kernels, plan_blocks(): pl.pallas_call(functools.partial(plan_body, layout=layout, row_slots=row_...  20.5 us
    pallas_call x2, Pallas kernels, grid_part(): pl.pallas_call(functools.partial(grid_body, part=part, first_part=first_p...  10.6 us
    pallas_call x1, Pallas kernels, make_kernels(): pl.pallas_call(kernels_body, in_specs=[hbm] * 5, out_specs=pl.BlockSpec(m...  8.6 us
    all_to_all x1, starting transfers between devices, shards(): lax.all_to_all(outgoing, both, split_axis=0, concat_axis=0, tiled=True)  7.3 us
    all_to_all x1, waiting for transfers between devices, shards(): lax.all_to_all(outgoing, both, split_axis=0, concat_axis=0, tiled=True)  5.09 us
    ppermute x3, starting transfers between devices, around(): return lax.ppermute(block, axes, route)  4 us
  transfers between devices with their start and end apart: 4, of which 1 were waited for; matrix products, arithmetic and copies ran while one was open for 0% of the time, Pallas kernels for 44%

profile of v10, /device:TPU:0, one launch (start us, length us, event | category | flops | bytes accessed | tf_op | source)
XLA Modules:
  0.0 58.0 jit_solution(7855713922682591564)
XLA Ops:
  0.0 0.0 copy-start
  0.0 0.0 copy-start.1
  0.0 8.6 %make_kernels.1 = bf16[64,64,128]{2,1,0:T(8,128)(2,1)} custom-call(s32[2,32]{1,0:T(2,128)} %bitcast.7, s32[1,32]{1,0:T(1,128)} %count_hbm.1, f32[4]{0:T(128)} %depth_hbm.1, bf16[4,512,512]{2,1,0:T(8,128)(2,1)} %amp_hbm.1, bf16[4,512,512]{2,1,0:T(8,128)(2,1)} %phase_hbm.1), custom_call_target="tpu_custom_call" | custom-call | tf_op jit(solution)/shard_map/make_kernels/pallas_call | solution.py:157
  8.6 7.3 %all-to-all-start = ((bf16[32,2,64,128]{3,2,1,0:T(8,128)(2,1)}), bf16[32,2,64,128]{3,2,1,0:T(8,128)(2,1)S(1)}, u32[]{:S(2)}, u32[]{:S(2)}) async-start(bf16[32,2,64,128]{3,2,1,0:T(8,128)(2,1)} %bitcast.2), calls=%async_computation | async-start | bytes 2097152 | tf_op jit(solution)/shard_map/all_to_all | solution.py:560
  16.6 0.0 copy-done
  16.6 0.0 copy-done.1
  16.6 20.5 %plan_blocks.1 = (s32[675]{0:T(1024)S(4)}, bf16[512,128,128]{2,1,0:T(8,128)(2,1)}, bf16[512,64,128]{2,1,0:T(8,128)(2,1)}) custom-call(s32[384]{0:T(512)S(1)} %copy-done, s32[384]{0:T(512)S(1)} %copy-done.1, s32[1]{0:T(128)S(6)} %copy.19.count_ref, bf16[384,128,128]{2,1,0:T(8,128)(2,1)} %left_hbm.1, bf16[384,64,128]{2,1,0:T(8,128)(2,1)} %right_hbm.1), custom_call_target="tpu_custom_call" | custom-call | tf_op jit(solution)/shard_map/plan_blocks/pallas_call | solution.py:304
  37.1 5.1 %all-to-all-done = bf16[32,2,64,128]{3,2,1,0:T(8,128)(2,1)S(1)} async-done(((bf16[32,2,64,128]{3,2,1,0:T(8,128)(2,1)}), bf16[32,2,64,128]{3,2,1,0:T(8,128)(2,1)S(1)}, u32[]{:S(2)}, u32[]{:S(2)}) %all-to-all-start) | async-done | bytes 1048608 | tf_op jit(solution)/shard_map/all_to_all | solution.py:560
  42.2 5.3 %grid_part.2 = (f32[32,128,256]{2,1,0:T(8,128)S(1)}, bf16[4,64,128,128]{3,2,1,0:T(8,128)(2,1)S(1)}, bf16[4,64,64,128]{3,2,1,0:T(8,128)(2,1)S(1)}, bf16[8,512,256...) custom-call(s32[675]{0:T(1024)S(4)} %get-tuple-element.16.plan_ref, ...), custom_call_target="tpu_custom_call" | custom-call | tf_op jit(solution)/shard_map/grid_part/pallas_call | solution.py:474
  47.5 1.5 %collective-permute-start = (bf16[2,64,512]{2,1,0:T(8,128)(2,1)S(1)}, bf16[2,64,512]{2,1,0:T(8,128)(2,1)S(1)}, u32[]{:S(2)}, u32[]{:S(2)}) collective-permute-start(bf16[2,64,512]{2,1,0:T(8,128)(2,1)S(1)} %get-tuple-element.24), channel_id=1, source_target_pairs={{0,4},{4,8},{8,12},{12,16},{16,20},{20,24},{24,28},{28,0},{1,5},{5... | collective-permute-start | bytes 393224 | tf_op jit(solution)/shard_map/ppermute | solution.py:49
  49.0 0.0 collective-permute-start.1
  49.0 2.5 %collective-permute-start.2 = (bf16[64,128]{1,0:T(8,128)(2,1)S(1)}, bf16[64,128]{1,0:T(8,128)(2,1)S(1)}, u32[]{:S(2)}, u32[]{:S(2)}) collective-permute-start(bf16[64,128]{1,0:T(8,128)(2,1)S(1)} %get-tuple-element.26), channel_id=1, source_target_pairs={{0,5},{1,6},{2,7},{3,4},{4,9},{5,10},{6,11},{7,8},{8,13},{9,14},{1... | collective-permute-start | bytes 49160 | tf_op jit(solution)/shard_map/ppermute | solution.py:49
  51.5 5.3 %grid_part.3 = (f32[32,128,256]{2,1,0:T(8,128)S(1)}, bf16[4,64,128,128]{3,2,1,0:T(8,128)(2,1)S(1)}, bf16[4,64,64,128]{3,2,1,0:T(8,128)(2,1)S(1)}, bf16[8,512,256]{2,1,0:T(8,128)(2,1)S(1)}) custom-call(s32[675]{0:T(1024)S(4)} %get-tuple-element.16.plan_ref, ...), custom_call_target="tpu_custom_call", output_to_operand_aliasing={{0}: (4, {}), {1}: (5, {}), {2}: (6, {}), {3}: (7, {})} | custom-call | tf_op jit(solution)/shard_map/grid_part/pallas_call | solution.py:474
  56.8 0.0 collective-permute-done.2.corner_ref
  56.8 0.0 collective-permute-done.1.col_ref
  56.8 0.0 collective-permute-done.row_ref
  56.8 1.1 %merge_tile.1 = f32[2,256,512]{2,1,0:T(8,128)} custom-call(f32[32,128,256]{2,1,0:T(8,128)S(1)} %get-tuple-element.23.sums, bf16[2,64,512]{2,1,0:T(8,128)(2,1)S(1)} %collective-permute-done.row_ref, bf16[256,128]{1,0:T(8,128)(2,1)S(1)} %collective-permute-done.1.col_ref, bf16[64,128]{1,0:T(8,128)(2,1)S(1)} %collective-permute-done.2.corner_ref), custom_call_target="tpu_custom_call" | custom-call | tf_op jit(solution)/shard_map/merge_tile/pallas_call | solution.py:527
Async XLA Ops:
  0.0 16.6 %copy-start = (s32[384]{0:T(512)S(1)}, s32[384]{0:T(512)}, u32[]{:S(2)}) copy-start(s32[384]{0:T(512)} %pos_ref.1) | copy-start | bytes 4612
  0.0 16.6 %copy-start.1 = (s32[384]{0:T(512)S(1)}, s32[384]{0:T(512)}, u32[]{:S(2)}) copy-start(s32[384]{0:T(512)} %slot_ref.1) | copy-start | bytes 4612
  8.6 33.5 %all-to-all-start = ((bf16[32,2,64,128]{3,2,1,0:T(8,128)(2,1)}), bf16[32,2,64,128]{3,2,1,0:T(8,128)(2,1)S(1)}, u32[]{:S(2)}, u32[]{:S(2)}) async-start(bf16[32,2,64,128]{3,2,1,0:T(8,128)(2,1)} %bitcast.2), calls=%async_computation | async-start | bytes 2097152 | tf_op jit(solution)/shard_map/all_to_all | solution.py:560
  47.5 9.3 %collective-permute-start = (bf16[2,64,512]{2,1,0:T(8,128)(2,1)S(1)}, bf16[2,64,512]{2,1,0:T(8,128)(2,1)S(1)}, u32[]{:S(2)}, u32[]{:S(2)}) collective-permute-start(bf16[2,64,512]{2,1,0:T(8,128)(2,1)S(1)} %get-tuple-element.24), channel_id=1, source_target_pairs={{0,4},{4,8},{8,12},{12,16},{16,20},{20,24},{24,28},{28,0},{1,5},{5... | collective-permute-start | bytes 393224 | tf_op jit(solution)/shard_map/ppermute | solution.py:49
  49.0 7.8 %collective-permute-start.1 = (bf16[256,128]{1,0:T(8,128)(2,1)S(1)}, bf16[256,128]{1,0:T(8,128)(2,1)S(1)}, u32[]{:S(2)}, u32[]{:S(2)}) collective-permute-start(bf16[256,128]{1,0:T(8,128)(2,1)S(1)} %get-tuple-element.25), channel_id=1, source_target_pairs={{0,1},{1,2},{2,3},{3,0},{4,5},{5,6},{6,7},{7,4},{8,9},{9,10},{10,1... | collective-permute-start | bytes 196616 | tf_op jit(solution)/shard_map/ppermute | solution.py:49
  49.0 7.8 %collective-permute-start.2 = (bf16[64,128]{1,0:T(8,128)(2,1)S(1)}, bf16[64,128]{1,0:T(8,128)(2,1)S(1)}, u32[]{:S(2)}, u32[]{:S(2)}) collective-permute-start(bf16[64,128]{1,0:T(8,128)(2,1)S(1)} %get-tuple-element.26), channel_id=1, source_target_pairs={{0,5},{1,6},{2,7},{3,4},{4,9},{5,10},{6,11},{7,8},{8,13},{9,14},{1... | collective-permute-start | bytes 49160 | tf_op jit(solution)/shard_map/ppermute | solution.py:49
